TPU v7x, 32 devices: a whole 2x2x4 slice. The times are simulated.
32 devices in a mesh: dp: 8 (over y, x, core), tensor: 4 (over z).
Axes of the slice: x: 2, y: 2, z: 4, core: 2. Of those that a mesh axis runs over, the one named last changes fastest.
Arguments:
- tokens: bfloat16 [2, 2048, 768], P(None, ('dp', 'tensor')), may hold values from -6 to 6
- encoder: bfloat16 [2, 1024, 768], P(None, ('dp', 'tensor')), may hold values from -6 to 6
- cotangent: bfloat16 [2, 2048, 768], P(None, ('dp', 'tensor')), may hold values from -6 to 6
- dec_segments: int32 [2, 8, 256], P(None, 'dp'), may hold values from 0 to 2, as said below
- enc_segments: int32 [2, 8, 128], P(None, 'dp'), may hold values from 0 to 2, as said below
- buckets: int32 [256], replicated, may hold values from 0 to 31, as said below
- self_query: bfloat16 [768, 768], P('dp', 'tensor'), may hold values from -0.046875 to 0.046875
- self_key: bfloat16 [768, 768], P('dp', 'tensor'), may hold values from -0.21875 to 0.21875
- self_value: bfloat16 [768, 768], P('dp', 'tensor'), may hold values from -0.21875 to 0.21875
- self_output: bfloat16 [768, 768], P('tensor', 'dp'), may hold values from -1.25 to 1.25
- cross_query: bfloat16 [768, 768], P('dp', 'tensor'), may hold values from -0.046875 to 0.046875
- cross_key: bfloat16 [768, 768], P('dp', 'tensor'), may hold values from -0.21875 to 0.21875
- cross_value: bfloat16 [768, 768], P('dp', 'tensor'), may hold values from -0.21875 to 0.21875
- cross_output: bfloat16 [768, 768], P('tensor', 'dp'), may hold values from -1.25 to 1.25
- gate_weight: bfloat16 [768, 2048], P('dp', 'tensor'), may hold values from -0.21875 to 0.21875
- up_weight: bfloat16 [768, 2048], P('dp', 'tensor'), may hold values from -0.21875 to 0.21875
- down_weight: bfloat16 [2048, 768], P('tensor', 'dp'), may hold values from -0.125 to 0.125
- gain_self: bfloat16 [768], P('dp'), may hold values from 0.5 to 1.5
- gain_cross: bfloat16 [768], P('dp'), may hold values from 0.5 to 1.5
- gain_feed: bfloat16 [768], P('dp'), may hold values from 0.5 to 1.5
- bias_table: bfloat16 [32, 12], P(None, 'tensor'), may hold values from -4 to 4
Outputs:
- layer_out: bfloat16 [2, 2048, 768], P(None, ('dp', 'tensor'))
- tokens_grad: float32 [2, 2048, 768], P(None, ('dp', 'tensor'))
- encoder_grad: float32 [2, 1024, 768], P(None, ('dp', 'tensor'))
- self_query_grad: float32 [768, 768], P('dp', 'tensor')
- self_key_grad: float32 [768, 768], P('dp', 'tensor')
- self_value_grad: float32 [768, 768], P('dp', 'tensor')
- self_output_grad: float32 [768, 768], P('tensor', 'dp')
- cross_query_grad: float32 [768, 768], P('dp', 'tensor')
- cross_key_grad: float32 [768, 768], P('dp', 'tensor')
- cross_value_grad: float32 [768, 768], P('dp', 'tensor')
- cross_output_grad: float32 [768, 768], P('tensor', 'dp')
- gate_weight_grad: float32 [768, 2048], P('dp', 'tensor')
- up_weight_grad: float32 [768, 2048], P('dp', 'tensor')
- down_weight_grad: float32 [2048, 768], P('tensor', 'dp')
- gain_self_grad: float32 [768], P(('dp', 'tensor'))
- gain_cross_grad: float32 [768], P(('dp', 'tensor'))
- gain_feed_grad: float32 [768], P(('dp', 'tensor'))
- bias_table_grad: float32 [32, 12], P(None, 'tensor')
Inputs may be any that keep to these rules, and one draw needn't show every extreme that they name: `dec_segments`: in each sequence the documents are numbered 0, 1, 2 in order; document 1 begins before position 64 and includes position 192. `enc_segments`: in each encoder row the documents are numbered 0, 1, 2 in order, each with one token or more; document 1 begins before position 64. buckets[d] is the bucket of distance d and never falls as d grows; buckets[d] = d for d < 16, and the last entry is 31.
All inputs are finite; a program needn't handle non-finite values.
Results may differ from a plain program's by a relative error of at most 0.025.
The roundings to bfloat16 on the way count: a program that leaves them out, or rounds other values in their place, can miss the bound.
Values may be sent and summed in bfloat16 or wider, within the bound.
A program may use at most 128 MiB of HBM per device.

v0:
```python
import jax
import jax.numpy as jnp
from jax import lax
from jax.sharding import PartitionSpec as P

BUCKETS = 32


EPS = 1e-06
NEG = -1e30


def dot_plain(left, right):
    return jnp.dot(left, right, preferred_element_type=jnp.float32)


def dot_left_t(left, right):
    return lax.dot_general(
        left, right, (((0,), (0,)), ((), ())), preferred_element_type=jnp.float32
    )


def dot_right_t(left, right):
    return lax.dot_general(
        left, right, (((1,), (1,)), ((), ())), preferred_element_type=jnp.float32
    )


def gelu_tanh(values):
    return jax.nn.gelu(values, approximate=True)


def rms_parts(values, gain_row):
    inv_root = lax.rsqrt(jnp.mean(values * values, axis=-1, keepdims=True) + EPS)
    normal = values * inv_root
    return (normal * gain_row, normal, inv_root)


def rms_back(grad_out, normal, inv_root, gain_row):
    scaled = grad_out * gain_row
    values_grad = inv_root * (scaled - normal * jnp.mean(scaled * normal, axis=-1, keepdims=True))
    return (values_grad, jnp.sum(grad_out * normal, axis=0))


def head_split(values, heads_local):
    return values.reshape(values.shape[0], heads_local, values.shape[1] // heads_local)


def masked_scores(query_rows, key_rows, heads_local, extra, allowed):
    scores = (
        jnp.einsum(
            "qhd,khd->hqk",
            head_split(query_rows, heads_local),
            head_split(key_rows, heads_local),
            preferred_element_type=jnp.float32,
        )
        + extra
    )
    return jnp.where(allowed[None], scores, NEG)


def attend_forward(query_rows, key_rows, value_rows, heads_local, extra, allowed):
    scores = masked_scores(query_rows, key_rows, heads_local, extra, allowed)
    biggest = jnp.max(scores, axis=-1, keepdims=True)
    log_total = biggest + jnp.log(jnp.sum(jnp.exp(scores - biggest), axis=-1, keepdims=True))
    probs_low = jnp.exp(scores - log_total).astype(jnp.bfloat16)
    mixed = jnp.einsum(
        "hqk,khd->qhd",
        probs_low,
        head_split(value_rows, heads_local),
        preferred_element_type=jnp.float32,
    )
    return (mixed.reshape(query_rows.shape[0], -1).astype(jnp.bfloat16), log_total)


def attend_backward(
    query_rows, key_rows, value_rows, heads_local, extra, allowed, log_total, mixed_grad
):
    scores = masked_scores(query_rows, key_rows, heads_local, extra, allowed)
    probs = jnp.exp(scores - log_total)
    grad_heads = head_split(mixed_grad, heads_local)
    query_heads = head_split(query_rows, heads_local)
    key_heads = head_split(key_rows, heads_local)
    prob_grad = jnp.einsum(
        "qhd,khd->hqk",
        grad_heads,
        head_split(value_rows, heads_local),
        preferred_element_type=jnp.float32,
    )
    score_low = (probs * (prob_grad - jnp.sum(probs * prob_grad, axis=-1, keepdims=True))).astype(
        jnp.bfloat16
    )
    query_grad = jnp.einsum(
        "hqk,khd->qhd", score_low, key_heads, preferred_element_type=jnp.float32
    )
    key_grad = jnp.einsum(
        "hqk,qhd->khd", score_low, query_heads, preferred_element_type=jnp.float32
    )
    value_grad = jnp.einsum(
        "hqk,qhd->khd", probs.astype(jnp.bfloat16), grad_heads, preferred_element_type=jnp.float32
    )
    return (
        query_grad.reshape(query_rows.shape[0], -1).astype(jnp.bfloat16),
        key_grad.reshape(key_rows.shape[0], -1).astype(jnp.bfloat16),
        value_grad.reshape(key_rows.shape[0], -1).astype(jnp.bfloat16),
        score_low,
    )


def toeplitz_bias(bucket_low, table_local):
    per_distance = jnp.dot(bucket_low, table_local, preferred_element_type=jnp.float32)
    length = per_distance.shape[0]
    reversed_rows = jnp.concatenate(
        [per_distance[::-1].T, jnp.zeros((per_distance.shape[1], length), jnp.float32)], axis=1
    )
    tiled_rows = jnp.tile(reversed_rows, (1, length))
    skewed = tiled_rows[:, : length * (2 * length - 1)].reshape(-1, length, 2 * length - 1)
    return skewed[:, :, length - 1 :]


def table_back(score_low, bucket_float):
    heads_local = score_low.shape[0]
    length = score_low.shape[1]
    padded = jnp.concatenate(
        [jnp.zeros((heads_local, length, length - 1), jnp.float32), score_low.astype(jnp.float32)],
        axis=2,
    )
    flat_rows = jnp.concatenate(
        [padded.reshape(heads_local, -1), jnp.zeros((heads_local, length), jnp.float32)], axis=1
    )
    folded = jnp.sum(flat_rows.reshape(heads_local, length, 2 * length), axis=1)
    per_distance = folded[:, :length][:, ::-1].T
    return dot_left_t(bucket_float, per_distance)


def spread_rows(values):
    return lax.all_gather(values, "tensor", axis=0, tiled=True)


def gather_grad(values):
    return lax.all_gather(values, "tensor", axis=0, tiled=True)


def add_parts(values):
    return lax.psum_scatter(values, "tensor", scatter_dimension=0, tiled=True)


def input_parts(values):
    return lax.psum_scatter(
        values.astype(jnp.bfloat16), "tensor", scatter_dimension=0, tiled=True
    ).astype(jnp.float32)


def body(
    tokens,
    encoder,
    cotangent,
    dec_segments,
    enc_segments,
    buckets,
    self_query,
    self_key,
    self_value,
    self_output,
    cross_query,
    cross_key,
    cross_value,
    cross_output,
    gate_weight,
    up_weight,
    down_weight,
    gain_self,
    gain_cross,
    gain_feed,
    bias_table,
):
    shards = (
        self_query,
        self_key,
        self_value,
        self_output,
        cross_query,
        cross_key,
        cross_value,
        cross_output,
        gate_weight,
        up_weight,
        down_weight,
        gain_self,
        gain_cross,
        gain_feed,
    )
    dp_count = lax.axis_size("dp")
    heads_local = bias_table.shape[1]
    seq_len = dec_segments.shape[2]
    position = jnp.arange(seq_len, dtype=jnp.int32)
    causal = position[:, None] >= position[None, :]
    bucket_hits = buckets[:, None] == jnp.arange(BUCKETS, dtype=jnp.int32)[None, :]
    bucket_float = bucket_hits.astype(jnp.float32)
    bias_full = toeplitz_bias(bucket_hits.astype(jnp.bfloat16), bias_table)
    left_parts = [[] for index_weight in range(11)]
    right_parts = [[] for index_weight in range(11)]
    gain_totals = [
        jnp.zeros((gain_self.shape[0] * dp_count,), jnp.float32) for index_gain in range(3)
    ]
    table_total = jnp.zeros((BUCKETS, heads_local), jnp.float32)
    outputs = []
    token_grads = []
    encoder_grads = []
    for micro_step in range(tokens.shape[0]):
        full = (
            lax.all_gather(shards[0], "dp", axis=0, tiled=True),
            lax.all_gather(shards[1], "dp", axis=0, tiled=True),
            lax.all_gather(shards[2], "dp", axis=0, tiled=True),
            lax.all_gather(shards[3], "dp", axis=1, tiled=True),
            lax.all_gather(shards[4], "dp", axis=0, tiled=True),
            lax.all_gather(shards[5], "dp", axis=0, tiled=True),
            lax.all_gather(shards[6], "dp", axis=0, tiled=True),
            lax.all_gather(shards[7], "dp", axis=1, tiled=True),
            lax.all_gather(shards[8], "dp", axis=0, tiled=True),
            lax.all_gather(shards[9], "dp", axis=0, tiled=True),
            lax.all_gather(shards[10], "dp", axis=1, tiled=True),
            lax.all_gather(shards[11], "dp", axis=0, tiled=True),
            lax.all_gather(shards[12], "dp", axis=0, tiled=True),
            lax.all_gather(shards[13], "dp", axis=0, tiled=True),
        )
        (
            q_self,
            k_self,
            v_self,
            o_self,
            q_cross,
            k_cross,
            v_cross,
            o_cross,
            gate_projection_weight,
            up_projection_weight,
            down_projection_weight,
            self_norm_gain,
            cross_norm_gain,
            feed_norm_gain,
        ) = full
        token_rows = tokens[micro_step].astype(jnp.float32)
        dec_seg = dec_segments[micro_step, 0]
        enc_seg = enc_segments[micro_step, 0]
        self_allowed = causal & (dec_seg[:, None] == dec_seg[None, :])
        cross_allowed = dec_seg[:, None] == enc_seg[None, :]
        self_normed_rows, normal1, inv1 = rms_parts(token_rows, self_norm_gain.astype(jnp.float32))
        normed1_all = spread_rows(self_normed_rows.astype(jnp.bfloat16))
        query1 = dot_plain(normed1_all, q_self).astype(jnp.bfloat16)
        self_key_heads = dot_plain(normed1_all, k_self).astype(jnp.bfloat16)
        value1 = dot_plain(normed1_all, v_self).astype(jnp.bfloat16)
        mixed1, total1 = attend_forward(
            query1, self_key_heads, value1, heads_local, bias_full, self_allowed
        )
        first = token_rows + add_parts(dot_plain(mixed1, o_self))
        normed2, normal2, inv2 = rms_parts(first, cross_norm_gain.astype(jnp.float32))
        normed2_all = spread_rows(normed2.astype(jnp.bfloat16))
        encoder_all = lax.all_gather(encoder[micro_step], "tensor", axis=0, tiled=True)
        query2 = dot_plain(normed2_all, q_cross).astype(jnp.bfloat16)
        key2 = dot_plain(encoder_all, k_cross).astype(jnp.bfloat16)
        value2 = dot_plain(encoder_all, v_cross).astype(jnp.bfloat16)
        mixed2, total2 = attend_forward(query2, key2, value2, heads_local, 0.0, cross_allowed)
        second = first + add_parts(dot_plain(mixed2, o_cross))
        normed3, normal3, inv3 = rms_parts(second, feed_norm_gain.astype(jnp.float32))
        normed3_all = spread_rows(normed3.astype(jnp.bfloat16))
        gate_pre = dot_plain(normed3_all, gate_projection_weight)
        up_pre = dot_plain(normed3_all, up_projection_weight)
        gate_act, gate_pull = jax.vjp(gelu_tanh, gate_pre)
        hidden = (gate_act * up_pre).astype(jnp.bfloat16)
        final = second + add_parts(dot_plain(hidden, down_projection_weight))
        outputs.append(final.astype(jnp.bfloat16))
        out_grad = cotangent[micro_step]
        down_grad_all = gather_grad(out_grad)
        hidden_grad = dot_right_t(down_grad_all, down_projection_weight)
        left_parts[10].append(hidden)
        right_parts[10].append(down_grad_all)
        gate_grad = gate_pull(hidden_grad * up_pre)[0].astype(jnp.bfloat16)
        up_grad = (hidden_grad * gate_act).astype(jnp.bfloat16)
        left_parts[8].append(normed3_all)
        right_parts[8].append(gate_grad)
        left_parts[9].append(normed3_all)
        right_parts[9].append(up_grad)
        normed3_grad = input_parts(
            dot_right_t(gate_grad, gate_projection_weight)
            + dot_right_t(up_grad, up_projection_weight)
        )
        back3, gain3 = rms_back(normed3_grad, normal3, inv3, feed_norm_gain.astype(jnp.float32))
        gain_totals[2] = gain_totals[2] + gain3
        second_grad = out_grad.astype(jnp.float32) + back3
        cross_out_all = gather_grad(second_grad.astype(jnp.bfloat16))
        left_parts[7].append(mixed2)
        right_parts[7].append(cross_out_all)
        mixed2_grad = dot_right_t(cross_out_all, o_cross).astype(jnp.bfloat16)
        query2_grad, key2_grad, value2_grad, score2_low = attend_backward(
            query2, key2, value2, heads_local, 0.0, cross_allowed, total2, mixed2_grad
        )
        left_parts[4].append(normed2_all)
        right_parts[4].append(query2_grad)
        left_parts[5].append(encoder_all)
        right_parts[5].append(key2_grad)
        left_parts[6].append(encoder_all)
        right_parts[6].append(value2_grad)
        normed2_grad, encoder_grad = (
            lax.psum_scatter(
                dot_right_t(query2_grad, q_cross).astype(jnp.bfloat16),
                "tensor",
                scatter_dimension=0,
                tiled=True,
            ).astype(jnp.float32),
            lax.psum_scatter(
                (dot_right_t(key2_grad, k_cross) + dot_right_t(value2_grad, v_cross)).astype(
                    jnp.bfloat16
                ),
                "tensor",
                scatter_dimension=0,
                tiled=True,
            ).astype(jnp.float32),
        )
        encoder_grads.append(encoder_grad)
        back2, gain2 = rms_back(normed2_grad, normal2, inv2, cross_norm_gain.astype(jnp.float32))
        gain_totals[1] = gain_totals[1] + gain2
        first_grad = second_grad + back2
        self_out_all = gather_grad(first_grad.astype(jnp.bfloat16))
        left_parts[3].append(mixed1)
        right_parts[3].append(self_out_all)
        mixed1_grad = dot_right_t(self_out_all, o_self).astype(jnp.bfloat16)
        query1_grad, key1_grad, value1_grad, score1_low = attend_backward(
            query1,
            self_key_heads,
            value1,
            heads_local,
            bias_full,
            self_allowed,
            total1,
            mixed1_grad,
        )
        table_total = table_total + table_back(score1_low, bucket_float)
        left_parts[0].append(normed1_all)
        right_parts[0].append(query1_grad)
        left_parts[1].append(normed1_all)
        right_parts[1].append(key1_grad)
        left_parts[2].append(normed1_all)
        right_parts[2].append(value1_grad)
        normed1_grad = input_parts(
            dot_right_t(query1_grad, q_self)
            + dot_right_t(key1_grad, k_self)
            + dot_right_t(value1_grad, v_self)
        )
        back1, gain1 = rms_back(normed1_grad, normal1, inv1, self_norm_gain.astype(jnp.float32))
        gain_totals[0] = gain_totals[0] + gain1
        token_grads.append(first_grad + back1)
    weight_totals = [
        dot_left_t(
            jnp.concatenate(left_parts[index_weight], axis=0),
            jnp.concatenate(right_parts[index_weight], axis=0),
        )
        for index_weight in range(11)
    ]
    weight_grads = (
        lax.psum_scatter(weight_totals[0], "dp", scatter_dimension=0, tiled=True),
        lax.psum_scatter(weight_totals[1], "dp", scatter_dimension=0, tiled=True),
        lax.psum_scatter(weight_totals[2], "dp", scatter_dimension=0, tiled=True),
        lax.psum_scatter(weight_totals[3], "dp", scatter_dimension=1, tiled=True),
        lax.psum_scatter(weight_totals[4], "dp", scatter_dimension=0, tiled=True),
        lax.psum_scatter(weight_totals[5], "dp", scatter_dimension=0, tiled=True),
        lax.psum_scatter(weight_totals[6], "dp", scatter_dimension=0, tiled=True),
        lax.psum_scatter(weight_totals[7], "dp", scatter_dimension=1, tiled=True),
        lax.psum_scatter(weight_totals[8], "dp", scatter_dimension=0, tiled=True),
        lax.psum_scatter(weight_totals[9], "dp", scatter_dimension=0, tiled=True),
        lax.psum_scatter(weight_totals[10], "dp", scatter_dimension=1, tiled=True),
    )
    gain_grads = (
        lax.psum_scatter(gain_totals[0], ("dp", "tensor"), scatter_dimension=0, tiled=True),
        lax.psum_scatter(gain_totals[1], ("dp", "tensor"), scatter_dimension=0, tiled=True),
        lax.psum_scatter(gain_totals[2], ("dp", "tensor"), scatter_dimension=0, tiled=True),
    )
    table_grad = lax.psum(table_total, "dp")
    return (
        (jnp.stack(outputs), jnp.stack(token_grads), jnp.stack(encoder_grads))
        + tuple(weight_grads)
        + tuple(gain_grads)
        + (table_grad,)
    )


def solution(mesh):
    placed = (
        P(None, ("dp", "tensor"), None),
        P(None, ("dp", "tensor"), None),
        P(None, ("dp", "tensor"), None),
        P(None, "dp", None),
        P(None, "dp", None),
        P(),
        P("dp", "tensor"),
        P("dp", "tensor"),
        P("dp", "tensor"),
        P("tensor", "dp"),
        P("dp", "tensor"),
        P("dp", "tensor"),
        P("dp", "tensor"),
        P("tensor", "dp"),
        P("dp", "tensor"),
        P("dp", "tensor"),
        P("tensor", "dp"),
        P("dp"),
        P("dp"),
        P("dp"),
        P(None, "tensor"),
    )
    return jax.shard_map(
        body,
        mesh=mesh,
        in_specs=placed,
        out_specs=(
            P(None, ("dp", "tensor"), None),
            P(None, ("dp", "tensor"), None),
            P(None, ("dp", "tensor"), None),
            P("dp", "tensor"),
            P("dp", "tensor"),
            P("dp", "tensor"),
            P("tensor", "dp"),
            P("dp", "tensor"),
            P("dp", "tensor"),
            P("dp", "tensor"),
            P("tensor", "dp"),
            P("dp", "tensor"),
            P("dp", "tensor"),
            P("tensor", "dp"),
            P(("dp", "tensor")),
            P(("dp", "tensor")),
            P(("dp", "tensor")),
            P(None, "tensor"),
        ),
        check_vma=False,
    )
```

profile of v0, /device:TPU:0, one launch (start us, length us, event | category | flops | bytes accessed | tf_op | source)
XLA Modules:
  0.0 1036.2 jit_solution(7641227227994360611)
XLA Ops:
  12.8 16.0 %all-reduce.12 = (bf16[768]{0:T(1024)(128)(2,1)S(1)}, bf16[768]{0:T(1024)(128)(2,1)}, bf16[768]{0:T(1024)(128)(2,1)}) all-reduce(bf16[768]{0:T(1024)(128)(2,1)S(1)} %dynamic-update-slice, bf16[768]{0:T(1024)(128)(2,1)S(1)} %dynamic-update-slice.1, bf16[768]{0:T(1024)(128)(2,1)S(1)} %dynamic-update-slice.2), channel_id=1, replica_groups=mesh['dp'=8,'tensor'=4] {'dp'}, use_global_device_ids=true, to_apply=%add.5 | all-reduce | flops 2304 | bytes 9216
  100.1 19.7 %all_gather.99 = bf16[256,768]{1,0:T(8,128)(2,1)S(1)} all-gather(bf16[64,768]{1,0:T(8,128)(2,1)S(1)} %copy-done.122), channel_id=1, replica_groups=mesh['dp'=8,'tensor'=4] {'tensor'}, dimensions={0}, use_global_device_ids=true | all-gather | bytes 491520 | tf_op jit(solution)/shard_map/all_gather | solution.py:137
  179.2 15.1 %all_gather.107 = bf16[256,768]{1,0:T(8,128)(2,1)S(1)} all-gather(bf16[64,768]{1,0:T(8,128)(2,1)S(1)} %multiply_convert_fusion.11), channel_id=1, replica_groups=mesh['dp'=8,'tensor'=4] {'tensor'}, dimensions={0}, use_global_device_ids=true | all-gather | bytes 491520 | tf_op jit(solution)/shard_map/all_gather | solution.py:137
  197.8 17.7 %all-gather.2 = bf16[1,256,768]{2,1,0:T(8,128)(2,1)} all-gather(bf16[1,64,768]{2,1,0:T(8,128)(2,1)S(1)} %get-tuple-element.65), channel_id=4, replica_groups=mesh['dp'=8,'tensor'=4] {'tensor'}, dimensions={1}, use_global_device_ids=true | all-gather | bytes 491520 | tf_op jit(solution)/shard_map/all_gather | solution.py:141
  268.8 20.8 %reduce-scatter.42.cloned.1.call-done = bf16[64,768]{1,0:T(8,128)(2,1)} async-done(((bf16[256,768]{1,0:T(8,128)(2,1)}), bf16[64,768]{1,0:T(8,128)(2,1)}) %reduce-scatter.42.cloned.1.call-update) | async-done | bytes 98320 | tf_op jit(solution)/shard_map/reduce_scatter | solution.py:149
  353.9 17.8 %all-gather.3 = bf16[1,256,768]{2,1,0:T(8,128)(2,1)} all-gather(bf16[1,64,768]{2,1,0:T(8,128)(2,1)} %get-tuple-element.66), channel_id=5, replica_groups=mesh['dp'=8,'tensor'=4] {'tensor'}, dimensions={1}, use_global_device_ids=true | all-gather | bytes 491520 | tf_op jit(solution)/shard_map/all_gather | solution.py:141
  404.9 15.6 %reduce-scatter.48.cloned.1.call-done = bf16[64,768]{1,0:T(8,128)(2,1)} async-done(((bf16[256,768]{1,0:T(8,128)(2,1)}), bf16[64,768]{1,0:T(8,128)(2,1)}) %reduce-scatter.48.cloned.1.call-update) | async-done | bytes 98320 | tf_op jit(solution)/shard_map/reduce_scatter | solution.py:149
  422.1 22.4 %reduce-scatter.34.cloned.1.call-done = f32[64,768]{1,0:T(8,128)} async-done(((f32[256,768]{1,0:T(8,128)}), f32[64,768]{1,0:T(8,128)}) %reduce-scatter.34.cloned.1.call-update) | async-done | bytes 196624 | tf_op jit(solution)/shard_map/reduce_scatter | solution.py:145
  444.5 25.0 %reduce-scatter.40.cloned.1.call-done = f32[64,768]{1,0:T(8,128)} async-done(((f32[256,768]{1,0:T(8,128)}), f32[64,768]{1,0:T(8,128)}) %reduce-scatter.40.cloned.1.call-update) | async-done | bytes 196624 | tf_op jit(solution)/shard_map/reduce_scatter | solution.py:145
  471.9 15.1 %all_gather.124 = bf16[256,768]{1,0:T(8,128)(2,1)S(1)} all-gather(bf16[64,768]{1,0:T(8,128)(2,1)S(1)} %get-tuple-element.60), channel_id=1, replica_groups=mesh['dp'=8,'tensor'=4] {'tensor'}, dimensions={0}, use_global_device_ids=true | all-gather | bytes 491520 | tf_op jit(solution)/shard_map/all_gather | solution.py:141
  494.9 17.3 %all_gather.122 = bf16[256,768]{1,0:T(8,128)(2,1)S(1)} all-gather(bf16[64,768]{1,0:T(8,128)(2,1)} %get-tuple-element.40), channel_id=1, replica_groups=mesh['dp'=8,'tensor'=4] {'tensor'}, dimensions={0}, use_global_device_ids=true | all-gather | bytes 491520 | tf_op jit(solution)/shard_map/all_gather | solution.py:141
  527.3 15.1 %all_gather.125 = bf16[256,768]{1,0:T(8,128)(2,1)S(1)} all-gather(bf16[64,768]{1,0:T(8,128)(2,1)S(1)} %get-tuple-element.42), channel_id=1, replica_groups=mesh['dp'=8,'tensor'=4] {'tensor'}, dimensions={0}, use_global_device_ids=true | all-gather | bytes 491520 | tf_op jit(solution)/shard_map/all_gather | solution.py:141
  591.5 21.3 %reduce-scatter.46.cloned.1.call-done = bf16[64,768]{1,0:T(8,128)(2,1)} async-done(((bf16[256,768]{1,0:T(8,128)(2,1)}), bf16[64,768]{1,0:T(8,128)(2,1)}) %reduce-scatter.46.cloned.1.call-update) | async-done | bytes 98320 | tf_op jit(solution)/shard_map/reduce_scatter | solution.py:149
  612.8 21.1 %reduce-scatter.52.cloned.1.call-done = bf16[64,768]{1,0:T(8,128)(2,1)} async-done(((bf16[256,768]{1,0:T(8,128)(2,1)}), bf16[64,768]{1,0:T(8,128)(2,1)}) %reduce-scatter.52.cloned.1.call-update) | async-done | bytes 98320 | tf_op jit(solution)/shard_map/reduce_scatter | solution.py:149
  635.2 38.7 %all-reduce.11 = (f32[768]{0:T(1024)S(1)}, f32[768]{0:T(1024)S(1)}, f32[768]{0:T(1024)S(1)}) all-reduce(f32[768]{0:T(1024)S(1)} %add.278, f32[768]{0:T(1024)S(1)} %add.279, f32[768]{0:T(1024)S(1)} %copy-done.152), channel_id=31, replica_groups=mesh['dp'=8,'tensor'=4] {'dp','tensor'}, use_global_device_ids=true, to_apply=%region_51.52.clone | all-reduce | flops 2304 | bytes 18432
  679.2 33.3 %reduce-scatter.74.cloned.1.call-done = f32[512,96]{0,1:T(8,128)} async-done(((f32[512,768]{0,1:T(8,128)}), f32[512,96]{0,1:T(8,128)}) %reduce-scatter.74.cloned.1.call-update) | async-done | bytes 196624 | tf_op jit(solution)/shard_map/reduce_scatter | solution.py:371
  712.5 42.2 %reduce-scatter.72.cloned.1.call-done = f32[96,512]{1,0:T(8,128)} async-done(((f32[768,512]{1,0:T(8,128)}), f32[96,512]{1,0:T(8,128)}) %reduce-scatter.72.cloned.1.call-update) | async-done | bytes 196624 | tf_op jit(solution)/shard_map/reduce_scatter | solution.py:370
  754.7 42.4 %reduce-scatter.70.cloned.1.call-done = f32[96,512]{1,0:T(8,128)} async-done(((f32[768,512]{1,0:T(8,128)}), f32[96,512]{1,0:T(8,128)}) %reduce-scatter.70.cloned.1.call-update) | async-done | bytes 196624 | tf_op jit(solution)/shard_map/reduce_scatter | solution.py:369
  797.0 38.6 %reduce-scatter.64.cloned.1.call-done = f32[96,192]{1,0:T(8,128)} async-done(((f32[768,192]{1,0:T(8,128)}), f32[96,192]{1,0:T(8,128)}) %reduce-scatter.64.cloned.1.call-update) | async-done | bytes 73744 | tf_op jit(solution)/shard_map/reduce_scatter | solution.py:365
  835.6 38.8 %reduce-scatter.68.cloned.1.call-done = f32[96,192]{1,0:T(8,128)} async-done(((f32[768,192]{1,0:T(8,128)}), f32[96,192]{1,0:T(8,128)}) %reduce-scatter.68.cloned.1.call-update) | async-done | bytes 73744 | tf_op jit(solution)/shard_map/reduce_scatter | solution.py:367
  874.4 38.7 %reduce-scatter.66.cloned.1.call-done = f32[96,192]{1,0:T(8,128)} async-done(((f32[768,192]{1,0:T(8,128)}), f32[96,192]{1,0:T(8,128)}) %reduce-scatter.66.cloned.1.call-update) | async-done | bytes 73744 | tf_op jit(solution)/shard_map/reduce_scatter | solution.py:366
  913.1 38.8 %reduce-scatter.58.cloned.1.call-done = f32[96,192]{1,0:T(8,128)} async-done(((f32[768,192]{1,0:T(8,128)}), f32[96,192]{1,0:T(8,128)}) %reduce-scatter.58.cloned.1.call-update) | async-done | bytes 73744 | tf_op jit(solution)/shard_map/reduce_scatter | solution.py:361
  951.8 38.6 %reduce-scatter.60.cloned.1.call-done = f32[96,192]{1,0:T(8,128)} async-done(((f32[768,192]{1,0:T(8,128)}), f32[96,192]{1,0:T(8,128)}) %reduce-scatter.60.cloned.1.call-update) | async-done | bytes 73744 | tf_op jit(solution)/shard_map/reduce_scatter | solution.py:362
  990.4 38.7 %reduce-scatter.62.cloned.1.call-done = f32[96,192]{1,0:T(8,128)} async-done(((f32[768,192]{1,0:T(8,128)}), f32[96,192]{1,0:T(8,128)}) %reduce-scatter.62.cloned.1.call-update) | async-done | bytes 73744 | tf_op jit(solution)/shard_map/reduce_scatter | solution.py:363
  (602 shorter events, 370.1 us)
Async XLA Ops:
  7.2 169.4 %reduce-scatter.36.cloned.1.call-start = ((), (), s32[]{:S(2)}) async-start(), calls=%async_computation.28 | async-start | bytes 983040 | tf_op jit(solution)/shard_map/reduce_scatter | solution.py:145
  100.0 76.7 %reduce-scatter.30.cloned.1.call-start = ((), (), s32[]{:S(2)}) async-start(), calls=%async_computation.25 | async-start | bytes 983040 | tf_op jit(solution)/shard_map/reduce_scatter | solution.py:145
  124.2 122.8 %reduce-scatter.32.cloned.1.call-start = ((), (), s32[]{:S(2)}) async-start(), calls=%async_computation.26 | async-start | bytes 983040 | tf_op jit(solution)/shard_map/reduce_scatter | solution.py:145
  197.1 92.5 %reduce-scatter.42.cloned.1.call-start = ((), (), s32[]{:S(2)}) async-start(), calls=%async_computation.31 | async-start | bytes 491520 | tf_op jit(solution)/shard_map/reduce_scatter | solution.py:149
  268.7 64.2 %reduce-scatter.44.cloned.1.call-start = ((), (), s32[]{:S(2)}) async-start(), calls=%async_computation.32 | async-start | bytes 491520 | tf_op jit(solution)/shard_map/reduce_scatter | solution.py:305
  312.4 66.5 %reduce-scatter.38.cloned.1.call-start = ((), (), s32[]{:S(2)}) async-start(), calls=%async_computation.29 | async-start | bytes 983040 | tf_op jit(solution)/shard_map/reduce_scatter | solution.py:145
  353.9 66.6 %reduce-scatter.48.cloned.1.call-start = ((), (), s32[]{:S(2)}) async-start(), calls=%async_computation.34 | async-start | bytes 491520 | tf_op jit(solution)/shard_map/reduce_scatter | solution.py:149
  402.8 66.8 %reduce-scatter.40.cloned.1.call-start = ((), (), s32[]{:S(2)}) async-start(), calls=%async_computation.30 | async-start | bytes 983040 | tf_op jit(solution)/shard_map/reduce_scatter | solution.py:145
  404.1 119.7 %reduce-scatter.50.cloned.1.call-start = ((), (), s32[]{:S(2)}) async-start(), calls=%async_computation.35 | async-start | bytes 491520 | tf_op jit(solution)/shard_map/reduce_scatter | solution.py:305
  489.7 79.9 %reduce-scatter.54.cloned.1.call-start = ((), (), s32[]{:S(2)}) async-start(), calls=%async_computation.37 | async-start | bytes 245760 | tf_op jit(solution)/shard_map/reduce_scatter | solution.py:311
  493.7 75.9 %reduce-scatter.56.cloned.1.call-start = ((), (), s32[]{:S(2)}) async-start(), calls=%async_computation.38 | async-start | bytes 245760 | tf_op jit(solution)/shard_map/reduce_scatter | solution.py:311
  515.7 74.1 %reduce-scatter.78.cloned.1.call-start = ((), (), s32[]{:S(2)}) async-start(), calls=%async_computation.49 | async-start | bytes 884736
  521.4 91.4 %reduce-scatter.46.cloned.1.call-start = ((), (), s32[]{:S(2)}) async-start(), calls=%async_computation.33 | async-start | bytes 491520 | tf_op jit(solution)/shard_map/reduce_scatter | solution.py:149
  523.8 110.1 %reduce-scatter.52.cloned.1.call-start = ((), (), s32[]{:S(2)}) async-start(), calls=%async_computation.36 | async-start | bytes 491520 | tf_op jit(solution)/shard_map/reduce_scatter | solution.py:149
  547.1 130.5 %reduce-scatter.76.cloned.1.call-start = ((), (), s32[]{:S(2)}) async-start(), calls=%async_computation.48 | async-start | bytes 884736
  548.5 163.9 %reduce-scatter.74.cloned.1.call-start = ((), (), s32[]{:S(2)}) async-start(), calls=%async_computation.47 | async-start | bytes 1769472 | tf_op jit(solution)/shard_map/reduce_scatter | solution.py:371
  550.4 204.2 %reduce-scatter.72.cloned.1.call-start = ((), (), s32[]{:S(2)}) async-start(), calls=%async_computation.46 | async-start | bytes 1769472 | tf_op jit(solution)/shard_map/reduce_scatter | solution.py:370
  553.4 243.6 %reduce-scatter.70.cloned.1.call-start = ((), (), s32[]{:S(2)}) async-start(), calls=%async_computation.45 | async-start | bytes 1769472 | tf_op jit(solution)/shard_map/reduce_scatter | solution.py:369
  555.3 280.3 %reduce-scatter.64.cloned.1.call-start = ((), (), s32[]{:S(2)}) async-start(), calls=%async_computation.42 | async-start | bytes 884736 | tf_op jit(solution)/shard_map/reduce_scatter | solution.py:365
  556.8 317.6 %reduce-scatter.68.cloned.1.call-start = ((), (), s32[]{:S(2)}) async-start(), calls=%async_computation.44 | async-start | bytes 884736 | tf_op jit(solution)/shard_map/reduce_scatter | solution.py:367
  558.3 354.8 %reduce-scatter.66.cloned.1.call-start = ((), (), s32[]{:S(2)}) async-start(), calls=%async_computation.43 | async-start | bytes 884736 | tf_op jit(solution)/shard_map/reduce_scatter | solution.py:366
  563.2 388.6 %reduce-scatter.58.cloned.1.call-start = ((), (), s32[]{:S(2)}) async-start(), calls=%async_computation.39 | async-start | bytes 884736 | tf_op jit(solution)/shard_map/reduce_scatter | solution.py:361
  566.4 424.1 %reduce-scatter.60.cloned.1.call-start = ((), (), s32[]{:S(2)}) async-start(), calls=%async_computation.40 | async-start | bytes 884736 | tf_op jit(solution)/shard_map/reduce_scatter | solution.py:362
  574.6 454.6 %reduce-scatter.62.cloned.1.call-start = ((), (), s32[]{:S(2)}) async-start(), calls=%async_computation.41 | async-start | bytes 884736 | tf_op jit(solution)/shard_map/reduce_scatter | solution.py:363
  (173 other events, 2815.6 us)
Sparse Core Ops, SparseCore 0:
  100.1 27.5 reduce-scatter.35
  130.1 22.3 reduce-scatter.29
  197.2 23.8 reduce-scatter.31
  268.9 20.6 reduce-scatter.41
  312.5 19.1 reduce-scatter.43
  354.0 24.8 reduce-scatter.37
  400.5 19.9 reduce-scatter.47
  422.9 21.5 reduce-scatter.33
  446.9 22.5 reduce-scatter.39
  489.9 21.5 reduce-scatter.49
  513.7 19.4 reduce-scatter.53
  556.0 33.4 reduce-scatter.77
  592.2 20.5 reduce-scatter.45
  615.0 18.8 reduce-scatter.51
  636.9 33.3 reduce-scatter.75
  674.0 38.4 reduce-scatter.73
  716.2 38.4 reduce-scatter.71
  758.5 38.4 reduce-scatter.69
  800.6 34.9 reduce-scatter.63
  839.3 34.9 reduce-scatter.67
  878.1 34.9 reduce-scatter.65
  916.8 34.9 reduce-scatter.57
  955.4 34.9 reduce-scatter.59
  994.2 34.9 reduce-scatter.61
  (1 shorter events, 17.4 us)
where the time goes:
time: 1050 us; the launch traced here: 1040 us
  waiting for transfers between devices  484 us (46%)
  blocking collectives  391 us (37%)
  matrix products  67.7 us (6%)
  local copies, waits for them, and re-layouts  38.6 us (4%)
  other arithmetic  36.4 us (3%)
  between operations  17.4 us (2%)
    all_gather x6, blocking collectives, gather_grad(): return lax.all_gather(values, 'tensor', axis=0, tiled=True)  97.9 us
    all_gather x6, blocking collectives, spread_rows(): return lax.all_gather(values, 'tensor', axis=0, tiled=True)  93.8 us
    reduce_scatter x4, waiting for transfers between devices, input_parts(): lax.psum_scatter(values.astype(jnp.bfloat16), 'tensor', scatter_dimension...  78.8 us
    unnamed x2, blocking collectives  54.7 us
    reduce_scatter x6, waiting for transfers between devices, add_parts(): return lax.psum_scatter(values, 'tensor', scatter_dimension=0, tiled=True)  54.6 us
    reduce_scatter x1, waiting for transfers between devices, body(): lax.psum_scatter(weight_totals[8], 'dp', scatter_dimension=0, tiled=True)  42.4 us
    reduce_scatter x1, waiting for transfers between devices, body(): lax.psum_scatter(weight_totals[9], 'dp', scatter_dimension=0, tiled=True)  42.2 us
    reduce_scatter x1, waiting for transfers between devices, body(): lax.psum_scatter(weight_totals[0], 'dp', scatter_dimension=0, tiled=True)  38.8 us
  transfers between devices with their start and end apart: 25, of which 16 were waited for; matrix products, arithmetic and copies ran while one was open for 7% of the time, Pallas kernels for 0%

commit v1 on v0

v1 whole, which is shorter than its diff:
```python
import functools

import jax
import jax.numpy as jnp
from jax import lax
from jax.experimental import pallas as pl
from jax.experimental.pallas import tpu as pltpu
from jax.sharding import PartitionSpec as P

BUCKETS = 32
EPS = 1e-06
NEG = -1e30
MESH = pl.DeviceIdType.MESH
CUBE = 8
VMEM_LIMIT = 56 * 1024 * 1024


def run_together(*streams):
    streams = list(streams)
    while streams:
        for stream in list(streams):
            try:
                next(stream)
            except StopIteration:
                streams.remove(stream)


def greet(pos, count, cube_me):
    barrier = pltpu.get_barrier_semaphore()

    @pl.when(pos > 0)
    def _():
        pl.semaphore_signal(barrier, inc=1, device_id={"tensor": pos - 1}, device_id_type=MESH)

    @pl.when(pos < count - 1)
    def _():
        pl.semaphore_signal(barrier, inc=1, device_id={"tensor": pos + 1}, device_id_type=MESH)

    waits = 2 - jnp.where(pos == 0, 1, 0) - jnp.where(pos == count - 1, 1, 0)
    if cube_me is not None:
        for flip in (1, 2, 4):
            pl.semaphore_signal(
                barrier, inc=1, device_id={"dp": cube_me ^ flip}, device_id_type=MESH
            )
        waits = waits + 3
    pl.semaphore_wait(barrier, waits)


def line_gather(pos, count, buf, send, recv):
    micro = buf.shape[0]
    rows = buf.shape[1] // count

    def piece(block, step):
        return buf.at[step, pl.ds(pl.multiple_of(block * rows, rows), rows)]

    def copy(block, step, target, way):
        return pltpu.make_async_remote_copy(
            src_ref=piece(block, step),
            dst_ref=piece(block, step),
            send_sem=send.at[way, block, step],
            recv_sem=recv.at[block, step],
            device_id={"tensor": target},
            device_id_type=MESH,
        )

    for hop in range(count):
        for step in range(micro):
            for way, target, block, can_send in (
                (0, pos + 1, pos - hop, pos < count - 1),
                (1, pos - 1, pos + hop, pos > 0),
            ):
                there = (block >= 0) & (block < count)

                if hop > 0:

                    @pl.when(there)
                    def _(block=block, step=step, way=way, target=target):
                        copy(block, step, target, way).wait_recv()

                if hop < count - 1:

                    @pl.when(there & can_send)
                    def _(block=block, step=step, way=way, target=target):
                        copy(block, step, target, way).start()

        yield
    for hop in range(count - 1):
        for step in range(micro):
            for way, target, block, can_send in (
                (0, pos + 1, pos - hop, pos < count - 1),
                (1, pos - 1, pos + hop, pos > 0),
            ):

                @pl.when((block >= 0) & (block < count) & can_send)
                def _(block=block, step=step, way=way, target=target):
                    copy(block, step, target, way).wait_send()


def line_scatter(pos, count, parts, got, staged, total, send, recv):
    micro = parts.shape[0]
    rows = parts.shape[1] // count

    def at(block):
        return pl.ds(pl.multiple_of(block * rows, rows), rows)

    def copy(block, step, target, way):
        return pltpu.make_async_remote_copy(
            src_ref=staged.at[way, step, at(block)],
            dst_ref=got.at[way, step, at(block)],
            send_sem=send.at[way, block, step],
            recv_sem=recv.at[way, block, step],
            device_id={"tensor": target},
            device_id_type=MESH,
        )

    def ways(hop):
        return (
            (0, pos + 1, pos + hop, pos + hop < count, pos > 0),
            (1, pos - 1, pos - hop, pos - hop >= 0, pos < count - 1),
        )

    for hop in range(count - 1, 0, -1):
        for step in range(micro):
            for way, target, block, there, has_input in ways(hop):

                @pl.when(there & has_input)
                def _(way=way, target=target, block=block, step=step):
                    copy(block, step, target, way).wait_recv()
                    staged[way, step, at(block)] = (
                        parts[step, at(block)].astype(jnp.float32)
                        + got[way, step, at(block)].astype(jnp.float32)
                    ).astype(staged.dtype)
                    copy(block, step, target, way).start()

                @pl.when(there & jnp.logical_not(has_input))
                def _(way=way, target=target, block=block, step=step):
                    staged[way, step, at(block)] = parts[step, at(block)]
                    copy(block, step, target, way).start()

        yield
    for step in range(micro):
        total[step] = parts[step, at(pos)].astype(jnp.float32)
        for way, target, block, there, has_input in ways(0):

            @pl.when(has_input)
            def _(way=way, target=target, step=step):
                copy(pos, step, target, way).wait_recv()
                total[step] = total[step] + got[way, step, at(pos)].astype(jnp.float32)

    for hop in range(count - 1, 0, -1):
        for step in range(micro):
            for way, target, block, there, has_input in ways(hop):

                @pl.when(there)
                def _(way=way, target=target, block=block, step=step):
                    copy(block, step, target, way).wait_send()


def cube_gather(me, buf, send, recv):
    half_rows = buf.shape[1] // 2

    def copy(block, half, flip, slot):
        piece = buf.at[block, pl.ds(half * half_rows, half_rows)]
        return pltpu.make_async_remote_copy(
            src_ref=piece,
            dst_ref=piece,
            send_sem=send.at[slot, half],
            recv_sem=recv.at[block, half],
            device_id={"dp": me ^ flip},
            device_id_type=MESH,
        )

    started = []

    def begin(block, half, flip):
        one = copy(block, half, flip, len(started) // 2 if half == 0 else len(started) // 2)
        one.start()
        started.append(one)

    firsts = ((2, 4), (4, 2))
    for half in range(2):
        begin(me, half, firsts[half][0])
    for half in range(2):
        begin(me, half, firsts[half][1])
    for half in range(2):
        begin(me, half, 1)
    yield
    for half in range(2):
        first, second = firsts[half]
        copy(me ^ first, half, first, 0).wait_recv()
        begin(me ^ first, half, second)
    for half in range(2):
        begin(me ^ firsts[half][0], half, 1)
    yield
    for half in range(2):
        copy(me ^ firsts[half][1], half, firsts[half][1], 0).wait_recv()
        begin(me ^ firsts[half][1], half, 1)
    yield
    for half in range(2):
        copy(me ^ 6, half, firsts[half][1], 0).wait_recv()
        begin(me ^ 6, half, 1)
    yield
    for other in (0, 2, 4, 6):
        for half in range(2):
            copy(me ^ 1 ^ other, half, 1, 0).wait_recv()
    for one in started:
        one.wait_send()


def cube_scatter(me, parts, got1, sums, got2, got3, total, send1, recv1, send2, recv2, send3, recv3):
    half_rows = parts.shape[1] // 2
    firsts = ((2, 4), (4, 2))

    def rows_of(half):
        return pl.ds(half * half_rows, half_rows)

    def one_copy(src, dst, send, recv, flip):
        return pltpu.make_async_remote_copy(
            src_ref=src,
            dst_ref=dst,
            send_sem=send,
            recv_sem=recv,
            device_id={"dp": me ^ flip},
            device_id_type=MESH,
        )

    first_copies = {}
    for slot in (3, 1, 2, 0):
        first_copies[slot] = one_copy(
            parts.at[me ^ 1 ^ (2 * slot)], got1.at[slot], send1.at[slot], recv1.at[slot], 1
        )
        first_copies[slot].start()
    yield
    second_copies = {}
    for slot in (3, 1, 2, 0):
        first_copies[slot].wait_recv()
        sums[slot] = (
            parts[me ^ (2 * slot)].astype(jnp.float32) + got1[slot].astype(jnp.float32)
        ).astype(sums.dtype)
        for half in range(2):
            first, second = firsts[half]
            if slot == 3 or slot == first // 2:
                goes = 1 if slot == 3 else 0
                second_copies[half, goes] = one_copy(
                    sums.at[slot, rows_of(half)],
                    got2.at[half, goes],
                    send2.at[half, goes],
                    recv2.at[half, goes],
                    first,
                )
                second_copies[half, goes].start()
    yield
    third_copies = {}
    for half in range(2):
        first, second = firsts[half]
        second_copies[half, 1].wait_recv()
        slot = second // 2
        sums[slot, rows_of(half)] = (
            sums[slot, rows_of(half)].astype(jnp.float32) + got2[half, 1].astype(jnp.float32)
        ).astype(sums.dtype)
        third_copies[half] = one_copy(
            sums.at[slot, rows_of(half)], got3.at[half], send3.at[half], recv3.at[half], second
        )
        third_copies[half].start()
    yield
    for half in range(2):
        second_copies[half, 0].wait_recv()
        total[rows_of(half)] = sums[0, rows_of(half)].astype(jnp.float32) + got2[half, 0].astype(
            jnp.float32
        )
    yield
    for half in range(2):
        third_copies[half].wait_recv()
        total[rows_of(half)] = total[rows_of(half)] + got3[half].astype(jnp.float32)
    for group in (first_copies, second_copies, third_copies):
        for one in group.values():
            one.wait_send()


def norm_forward(values, gain_row):
    inv_root = lax.rsqrt(jnp.mean(values * values, axis=-1, keepdims=True) + EPS)
    return values * inv_root * gain_row


def norm_backward(grad_out, values, gain_row):
    inv_root = lax.rsqrt(jnp.mean(values * values, axis=-1, keepdims=True) + EPS)
    normal = values * inv_root
    scaled = grad_out * gain_row
    values_grad = inv_root * (scaled - normal * jnp.mean(scaled * normal, axis=-1, keepdims=True))
    return (values_grad, jnp.sum(grad_out * normal, axis=0, keepdims=True))


def own_rows(pos, buf, count):
    rows = buf.shape[1] // count
    return pl.ds(pl.multiple_of(pos * rows, rows), rows)


def scatter_scratch(shape):
    return [
        pltpu.VMEM((2,) + shape, jnp.bfloat16),
        pltpu.VMEM((2,) + shape, jnp.bfloat16),
    ]


def scatter_sems(count, micro):
    return [
        pltpu.SemaphoreType.DMA((2, count, micro)),
        pltpu.SemaphoreType.DMA((2, count, micro)),
    ]


def gather_sems(count, micro):
    return [
        pltpu.SemaphoreType.DMA((2, count, micro)),
        pltpu.SemaphoreType.DMA((count, micro)),
    ]


def call(kernel, outs, scratch, ident, name, *args):
    return pl.pallas_call(
        kernel,
        out_shape=[jax.ShapeDtypeStruct(shape, kind) for shape, kind in outs],
        in_specs=[pl.BlockSpec(memory_space=pltpu.VMEM)] * len(args),
        out_specs=[pl.BlockSpec(memory_space=pltpu.VMEM)] * len(outs),
        scratch_shapes=scratch,
        compiler_params=pltpu.CompilerParams(
            collective_id=ident, has_side_effects=True, vmem_limit_bytes=VMEM_LIMIT
        ),
        name=name,
    )(*args)


def entry_kernel(count, with_cube, *refs):
    if with_cube:
        weights, refs = refs[0], refs[1:]
    rows_in, refs = refs[:3], refs[3:]
    if with_cube:
        weights_all, refs = refs[0], refs[1:]
    rows_out, refs = refs[:3], refs[3:]
    pos = lax.axis_index("tensor")
    me = lax.axis_index("dp") if with_cube else None
    for source, target in zip(rows_in, rows_out):
        for step in range(source.shape[0]):
            target[step, own_rows(pos, target, count)] = source[step]
    if with_cube:
        weights_all[me] = weights[...]
    greet(pos, count, me)
    streams = []
    if with_cube:
        streams.append(cube_gather(me, weights_all, refs[6], refs[7]))

    def lines():
        for which in range(3):
            yield from line_gather(
                pos, count, rows_out[which], refs[2 * which], refs[2 * which + 1]
            )

    run_together(*streams, lines())


def forward_kernel(
    count, parts, resid, gain, total_out, normed_all, got, staged, s_send, s_recv, g_send, g_recv
):
    pos = lax.axis_index("tensor")
    greet(pos, count, None)
    run_together(line_scatter(pos, count, parts, got, staged, total_out, s_send, s_recv))
    for step in range(parts.shape[0]):
        total = total_out[step] + resid[step].astype(jnp.float32)
        total_out[step] = total
        normed_all[step, own_rows(pos, normed_all, count)] = norm_forward(total, gain[...]).astype(
            jnp.bfloat16
        )
    run_together(line_gather(pos, count, normed_all, g_send, g_recv))


def back_kernel(
    count,
    side_kind,
    parts,
    side_parts,
    values,
    gain,
    grad_in,
    side_resid,
    grad_out,
    gathered,
    side_out,
    gain_out,
    got,
    staged,
    side_got,
    side_staged,
    side_total,
    s_send,
    s_recv,
    t_send,
    t_recv,
    g_send,
    g_recv,
):
    pos = lax.axis_index("tensor")
    greet(pos, count, None)

    def main():
        yield from line_scatter(pos, count, parts, got, staged, grad_out, s_send, s_recv)
        gain_out[...] = jnp.zeros_like(gain_out)
        for step in range(parts.shape[0]):
            moved, gain_part = norm_backward(grad_out[step], values[step], gain[...])
            total = grad_in[step].astype(jnp.float32) + moved
            grad_out[step] = total
            gain_out[...] = gain_out[...] + gain_part
            gathered[step, own_rows(pos, gathered, count)] = total.astype(jnp.bfloat16)
        yield from line_gather(pos, count, gathered, g_send, g_recv)

    def side():
        yield from line_scatter(
            pos, count, side_parts, side_got, side_staged, side_total, t_send, t_recv
        )
        for step in range(parts.shape[0]):
            if side_kind == "out":
                side_out[step] = (side_total[step] + side_resid[step]).astype(jnp.bfloat16)
            else:
                side_out[step] = side_total[step]

    run_together(main(), side())


def exit_kernel(count, with_cube, *refs):
    parts, values, gain, grad_in = refs[:4]
    refs = refs[4:]
    if with_cube:
        weight_parts, refs = refs[0], refs[1:]
    grad_out, gain_out = refs[:2]
    refs = refs[2:]
    if with_cube:
        weight_out, refs = refs[0], refs[1:]
    got, staged, s_send, s_recv = refs[:4]
    refs = refs[4:]
    pos = lax.axis_index("tensor")
    me = lax.axis_index("dp") if with_cube else None
    greet(pos, count, me)

    def main():
        yield from line_scatter(pos, count, parts, got, staged, grad_out, s_send, s_recv)
        gain_out[...] = jnp.zeros_like(gain_out)
        for step in range(parts.shape[0]):
            moved, gain_part = norm_backward(
                grad_out[step], values[step].astype(jnp.float32), gain[...]
            )
            grad_out[step] = grad_in[step] + moved
            gain_out[...] = gain_out[...] + gain_part

    streams = [main()]
    if with_cube:
        got1, sums, got2, got3 = refs[:4]
        streams.insert(
            0, cube_scatter(me, weight_parts, got1, sums, got2, got3, weight_out, *refs[4:])
        )
    run_together(*streams)


def dot_plain(left, right):
    return jnp.dot(left, right, preferred_element_type=jnp.float32)


def dot_left_t(left, right):
    return lax.dot_general(
        left, right, (((0,), (0,)), ((), ())), preferred_element_type=jnp.float32
    )


def dot_right_t(left, right):
    return lax.dot_general(
        left, right, (((1,), (1,)), ((), ())), preferred_element_type=jnp.float32
    )


def gelu_tanh(values):
    return jax.nn.gelu(values, approximate=True)


def head_split(values, heads_local):
    return values.reshape(values.shape[:2] + (heads_local, values.shape[2] // heads_local))


def attend_forward(query_rows, key_rows, value_rows, heads_local, extra, allowed):
    scores = (
        jnp.einsum(
            "bqhd,bkhd->bhqk",
            head_split(query_rows, heads_local),
            head_split(key_rows, heads_local),
            preferred_element_type=jnp.float32,
        )
        + extra
    )
    scores = jnp.where(allowed[:, None], scores, NEG)
    biggest = jnp.max(scores, axis=-1, keepdims=True)
    exponent = jnp.exp(scores - biggest)
    probs = exponent / jnp.sum(exponent, axis=-1, keepdims=True)
    mixed = jnp.einsum(
        "bhqk,bkhd->bqhd",
        probs.astype(jnp.bfloat16),
        head_split(value_rows, heads_local),
        preferred_element_type=jnp.float32,
    )
    return (mixed.reshape(query_rows.shape).astype(jnp.bfloat16), probs)


def attend_backward(query_rows, key_rows, value_rows, heads_local, probs, mixed_grad):
    grad_heads = head_split(mixed_grad, heads_local)
    query_heads = head_split(query_rows, heads_local)
    key_heads = head_split(key_rows, heads_local)
    prob_grad = jnp.einsum(
        "bqhd,bkhd->bhqk",
        grad_heads,
        head_split(value_rows, heads_local),
        preferred_element_type=jnp.float32,
    )
    score_low = (probs * (prob_grad - jnp.sum(probs * prob_grad, axis=-1, keepdims=True))).astype(
        jnp.bfloat16
    )
    query_grad = jnp.einsum(
        "bhqk,bkhd->bqhd", score_low, key_heads, preferred_element_type=jnp.float32
    )
    key_grad = jnp.einsum(
        "bhqk,bqhd->bkhd", score_low, query_heads, preferred_element_type=jnp.float32
    )
    value_grad = jnp.einsum(
        "bhqk,bqhd->bkhd", probs.astype(jnp.bfloat16), grad_heads, preferred_element_type=jnp.float32
    )
    return (
        query_grad.reshape(query_rows.shape).astype(jnp.bfloat16),
        key_grad.reshape(key_rows.shape).astype(jnp.bfloat16),
        value_grad.reshape(key_rows.shape).astype(jnp.bfloat16),
        score_low,
    )


def rows_dot(rows, matrix):
    return lax.dot_general(
        rows, matrix, (((2,), (0,)), ((), ())), preferred_element_type=jnp.float32
    )


def rows_dot_t(rows, matrix):
    return lax.dot_general(
        rows, matrix, (((2,), (1,)), ((), ())), preferred_element_type=jnp.float32
    )


def weight_dot(left, right):
    return dot_left_t(
        left.reshape(-1, left.shape[-1]), right.reshape(-1, right.shape[-1])
    ).astype(jnp.bfloat16)

def toeplitz_bias(bucket_low, table_local):
    per_distance = jnp.dot(bucket_low, table_local, preferred_element_type=jnp.float32)
    length = per_distance.shape[0]
    reversed_rows = jnp.concatenate(
        [per_distance[::-1].T, jnp.zeros((per_distance.shape[1], length), jnp.float32)], axis=1
    )
    tiled_rows = jnp.tile(reversed_rows, (1, length))
    skewed = tiled_rows[:, : length * (2 * length - 1)].reshape(-1, length, 2 * length - 1)
    return skewed[:, :, length - 1 :]


def table_back(score_low, bucket_float):
    heads_local = score_low.shape[0]
    length = score_low.shape[1]
    padded = jnp.concatenate(
        [jnp.zeros((heads_local, length, length - 1), jnp.float32), score_low.astype(jnp.float32)],
        axis=2,
    )
    flat_rows = jnp.concatenate(
        [padded.reshape(heads_local, -1), jnp.zeros((heads_local, length), jnp.float32)], axis=1
    )
    folded = jnp.sum(flat_rows.reshape(heads_local, length, 2 * length), axis=1)
    per_distance = folded[:, :length][:, ::-1].T
    return dot_left_t(bucket_float, per_distance)


def body(
    tokens,
    encoder,
    cotangent,
    dec_segments,
    enc_segments,
    buckets,
    self_query,
    self_key,
    self_value,
    self_output,
    cross_query,
    cross_key,
    cross_value,
    cross_output,
    gate_weight,
    up_weight,
    down_weight,
    gain_self,
    gain_cross,
    gain_feed,
    bias_table,
):
    low = jnp.bfloat16
    dp_count = lax.axis_size("dp")
    count = lax.axis_size("tensor")
    heads_local = bias_table.shape[1]
    inner = self_query.shape[1]
    hidden_local = gate_weight.shape[1]
    shard_rows = self_query.shape[0]
    width = shard_rows * dp_count
    micro, row_count = tokens.shape[:2]
    seq_len = row_count * count
    enc_len = encoder.shape[1] * count
    with_cube = dp_count == CUBE and shard_rows % 32 == 0

    gain_columns = jnp.pad(
        jnp.stack([gain_self, gain_cross, gain_feed], axis=1), ((0, 0), (0, 125))
    )
    packed = jnp.concatenate(
        [
            gate_weight,
            up_weight,
            down_weight.T,
            self_query,
            self_key,
            self_value,
            cross_query,
            cross_key,
            cross_value,
            self_output.T,
            cross_output.T,
            gain_columns,
        ],
        axis=1,
    )
    rows_shape = (micro, seq_len, width)
    enc_shape = (micro, enc_len, width)
    own_shape = (micro, row_count, width)
    line_sems = gather_sems(count, micro)
    entry_args = [tokens, cotangent, encoder]
    entry_outs = [(rows_shape, low), (rows_shape, low), (enc_shape, low)]
    entry_scratch = line_sems * 3
    if with_cube:
        entry_args.insert(0, packed)
        entry_outs.insert(0, ((CUBE,) + packed.shape, low))
        entry_scratch = entry_scratch + [
            pltpu.SemaphoreType.DMA((8, 2)),
            pltpu.SemaphoreType.DMA((CUBE, 2)),
        ]
    entry = call(
        functools.partial(entry_kernel, count, with_cube),
        entry_outs,
        entry_scratch,
        0,
        "entry_gather",
        *entry_args,
    )
    if with_cube:
        whole, tokens_all, cot_all, encoder_all = entry
        whole = whole.reshape(width, packed.shape[1])
    else:
        tokens_all, cot_all, encoder_all = entry
        whole = lax.all_gather(packed, "dp", axis=0, tiled=True)
    w_gate_up = whole[:, : 2 * hidden_local]
    w_down_t = whole[:, 2 * hidden_local : 3 * hidden_local]
    base = 3 * hidden_local
    w_qkv = whole[:, base : base + 3 * inner]
    w_cq = whole[:, base + 3 * inner : base + 4 * inner]
    w_ckv = whole[:, base + 4 * inner : base + 6 * inner]
    w_so_t = whole[:, base + 6 * inner : base + 7 * inner]
    w_co_t = whole[:, base + 7 * inner : base + 8 * inner]
    gains = whole[:, base + 8 * inner : base + 8 * inner + 3].T.astype(jnp.float32)
    gain1, gain2, gain3 = gains[0:1], gains[1:2], gains[2:3]

    position = jnp.arange(seq_len, dtype=jnp.int32)
    causal = position[:, None] >= position[None, :]
    bucket_hits = buckets[:, None] == jnp.arange(BUCKETS, dtype=jnp.int32)[None, :]
    bias_full = toeplitz_bias(bucket_hits.astype(low), bias_table)
    dec_seg = dec_segments[:, 0]
    enc_seg = enc_segments[:, 0]
    self_allowed = causal[None] & (dec_seg[:, :, None] == dec_seg[:, None, :])
    cross_allowed = dec_seg[:, :, None] == enc_seg[:, None, :]

    forward_scratch = (
        scatter_scratch(rows_shape) + scatter_sems(count, micro) + gather_sems(count, micro)
    )
    normed1_all = norm_forward(tokens_all.astype(jnp.float32), gain1).astype(low)
    qkv = rows_dot(normed1_all, w_qkv).astype(low)
    query1, key1, value1 = (
        qkv[..., :inner],
        qkv[..., inner : 2 * inner],
        qkv[..., 2 * inner :],
    )
    mixed1, probs1 = attend_forward(query1, key1, value1, heads_local, bias_full, self_allowed)
    first, normed2_all = call(
        functools.partial(forward_kernel, count),
        [(own_shape, jnp.float32), (rows_shape, low)],
        forward_scratch,
        1,
        "self_sum_norm",
        rows_dot_t(mixed1, w_so_t).astype(low),
        tokens,
        gain2,
    )
    key_value2 = rows_dot(encoder_all, w_ckv).astype(low)
    key2, value2 = key_value2[..., :inner], key_value2[..., inner:]
    query2 = rows_dot(normed2_all, w_cq).astype(low)
    mixed2, probs2 = attend_forward(query2, key2, value2, heads_local, 0.0, cross_allowed)
    second, normed3_all = call(
        functools.partial(forward_kernel, count),
        [(own_shape, jnp.float32), (rows_shape, low)],
        forward_scratch,
        2,
        "cross_sum_norm",
        rows_dot_t(mixed2, w_co_t).astype(low),
        first,
        gain3,
    )
    gate_up = rows_dot(normed3_all, w_gate_up)
    gate_pre, up_pre = gate_up[..., :hidden_local], gate_up[..., hidden_local:]
    gate_act, gate_pull = jax.vjp(gelu_tanh, gate_pre)
    hidden = (gate_act * up_pre).astype(low)
    hidden_grad = rows_dot(cot_all, w_down_t)
    gate_grad = gate_pull(hidden_grad * up_pre)[0].astype(low)
    up_grad = (hidden_grad * gate_act).astype(low)
    gate_up_grad = jnp.concatenate([gate_grad, up_grad], axis=-1)

    def back_scratch(side_shape, side_own):
        return (
            scatter_scratch(rows_shape)
            + scatter_scratch(side_shape)
            + [pltpu.VMEM(side_own, jnp.float32)]
            + scatter_sems(count, micro) * 2
            + gather_sems(count, micro)
        )

    second_grad, cross_out_all, layer_out, gain3_part = call(
        functools.partial(back_kernel, count, "out"),
        [
            (own_shape, jnp.float32),
            (rows_shape, low),
            (own_shape, low),
            ((1, width), jnp.float32),
        ],
        back_scratch(rows_shape, own_shape),
        3,
        "feed_back",
        rows_dot_t(gate_up_grad, w_gate_up).astype(low),
        rows_dot_t(hidden, w_down_t).astype(low),
        second,
        gain3,
        cotangent,
        second,
    )
    mixed2_grad = rows_dot(cross_out_all, w_co_t).astype(low)
    query2_grad, key2_grad, value2_grad, score2_low = attend_backward(
        query2, key2, value2, heads_local, probs2, mixed2_grad
    )
    key_value2_grad = jnp.concatenate([key2_grad, value2_grad], axis=-1)
    enc_own = (micro, encoder.shape[1], width)
    first_grad, self_out_all, encoder_grad, gain2_part = call(
        functools.partial(back_kernel, count, "plain"),
        [
            (own_shape, jnp.float32),
            (rows_shape, low),
            (enc_own, jnp.float32),
            ((1, width), jnp.float32),
        ],
        back_scratch(enc_shape, enc_own),
        4,
        "cross_back",
        rows_dot_t(query2_grad, w_cq).astype(low),
        rows_dot_t(key_value2_grad, w_ckv).astype(low),
        first,
        gain2,
        second_grad,
        second,
    )
    mixed1_grad = rows_dot(self_out_all, w_so_t).astype(low)
    query1_grad, key1_grad, value1_grad, score1_low = attend_backward(
        query1, key1, value1, heads_local, probs1, mixed1_grad
    )
    qkv_grad = jnp.concatenate([query1_grad, key1_grad, value1_grad], axis=-1)
    weight_parts = jnp.concatenate(
        [
            weight_dot(normed3_all, gate_up_grad),
            weight_dot(cot_all, hidden),
            weight_dot(normed1_all, qkv_grad),
            weight_dot(normed2_all, query2_grad),
            weight_dot(encoder_all, key_value2_grad),
            weight_dot(self_out_all, mixed1),
            weight_dot(cross_out_all, mixed2),
        ],
        axis=1,
    )
    columns = weight_parts.shape[1]
    exit_args = [rows_dot_t(qkv_grad, w_qkv).astype(low), tokens, gain1, first_grad]
    exit_outs = [(own_shape, jnp.float32), ((1, width), jnp.float32)]
    exit_scratch = scatter_scratch(rows_shape) + scatter_sems(count, micro)
    if with_cube:
        exit_args.append(weight_parts.reshape(CUBE, shard_rows, columns))
        exit_outs.append(((shard_rows, columns), jnp.float32))
        exit_scratch = exit_scratch + [
            pltpu.VMEM((4, shard_rows, columns), low),
            pltpu.VMEM((4, shard_rows, columns), low),
            pltpu.VMEM((2, 2, shard_rows // 2, columns), low),
            pltpu.VMEM((2, shard_rows // 2, columns), low),
            pltpu.SemaphoreType.DMA((4,)),
            pltpu.SemaphoreType.DMA((4,)),
            pltpu.SemaphoreType.DMA((2, 2)),
            pltpu.SemaphoreType.DMA((2, 2)),
            pltpu.SemaphoreType.DMA((2,)),
            pltpu.SemaphoreType.DMA((2,)),
        ]
    ended = call(
        functools.partial(exit_kernel, count, with_cube),
        exit_outs,
        exit_scratch,
        5,
        "exit_sums",
        *exit_args,
    )
    if with_cube:
        token_grad, gain1_part, owned = ended
    else:
        token_grad, gain1_part = ended
        owned = lax.psum_scatter(
            weight_parts.astype(jnp.float32), "dp", scatter_dimension=0, tiled=True
        )
    tables = table_back(jnp.sum(score1_low.astype(jnp.float32), axis=0), bucket_hits.astype(jnp.float32))
    pos = lax.axis_index("tensor")
    placed_table = jnp.where(
        (jnp.arange(count, dtype=jnp.int32) == pos)[:, None, None], tables[None], 0.0
    )
    small = jnp.concatenate(
        [
            gain1_part.reshape(-1),
            gain2_part.reshape(-1),
            gain3_part.reshape(-1),
            placed_table.reshape(-1),
        ]
    )
    small = lax.psum(small, ("dp", "tensor"))
    index = lax.axis_index("dp") * count + pos
    piece = width // (dp_count * count)
    gain_grads = tuple(
        lax.dynamic_slice(small, (which * width + index * piece,), (piece,)) for which in range(3)
    )
    table_size = tables.shape[0] * tables.shape[1]
    table_grad = lax.dynamic_slice(small, (3 * width + pos * table_size,), (table_size,)).reshape(
        tables.shape
    )

    def wide(start, size):
        return owned[:, start : start + size]

    return (
        layer_out,
        token_grad,
        encoder_grad,
        wide(base, inner),
        wide(base + inner, inner),
        wide(base + 2 * inner, inner),
        wide(base + 6 * inner, inner).T,
        wide(base + 3 * inner, inner),
        wide(base + 4 * inner, inner),
        wide(base + 5 * inner, inner),
        wide(base + 7 * inner, inner).T,
        wide(0, hidden_local),
        wide(hidden_local, hidden_local),
        wide(2 * hidden_local, hidden_local).T,
    ) + gain_grads + (table_grad,)


def solution(mesh):
    placed = (
        P(None, ("dp", "tensor"), None),
        P(None, ("dp", "tensor"), None),
        P(None, ("dp", "tensor"), None),
        P(None, "dp", None),
        P(None, "dp", None),
        P(),
        P("dp", "tensor"),
        P("dp", "tensor"),
        P("dp", "tensor"),
        P("tensor", "dp"),
        P("dp", "tensor"),
        P("dp", "tensor"),
        P("dp", "tensor"),
        P("tensor", "dp"),
        P("dp", "tensor"),
        P("dp", "tensor"),
        P("tensor", "dp"),
        P("dp"),
        P("dp"),
        P("dp"),
        P(None, "tensor"),
    )
    return jax.shard_map(
        body,
        mesh=mesh,
        in_specs=placed,
        out_specs=(
            P(None, ("dp", "tensor"), None),
            P(None, ("dp", "tensor"), None),
            P(None, ("dp", "tensor"), None),
            P("dp", "tensor"),
            P("dp", "tensor"),
            P("dp", "tensor"),
            P("tensor", "dp"),
            P("dp", "tensor"),
            P("dp", "tensor"),
            P("dp", "tensor"),
            P("tensor", "dp"),
            P("dp", "tensor"),
            P("dp", "tensor"),
            P("tensor", "dp"),
            P(("dp", "tensor")),
            P(("dp", "tensor")),
            P(("dp", "tensor")),
            P(None, "tensor"),
        ),
        check_vma=False,
    )
```

time: 1050 us -> 355 us (0.34); the launches traced: 1040 us -> 353 us
  waiting for transfers between devices: 484 us -> 0 us
  blocking collectives: 391 us -> 38.7 us
  Pallas kernels: 0 us -> 208 us
  other arithmetic: 36.4 us -> 10.5 us
  between operations: 17.4 us -> 1.31 us
  matrix products: 67.7 us -> 52.6 us
    reduce_scatter x23 -> x0, waiting for transfers between devices: 483 us -> none  [the longest x4 78.8 us: input_parts(): lax.psum_scatter(values.astype(jnp.bfloat16), 'tensor', scatter_dimension...]
    all_gather x25 -> x0, blocking collectives: 324 us -> none  [the longest x6 97.9 us: gather_grad(): return lax.all_gather(values, 'tensor', axis=0, tiled=True)]
    pallas_call x0 -> x6, Pallas kernels: none -> 208 us  [call(): pl.pallas_call(kernel, out_shape=[jax.ShapeDtypeStruct(shape, kind) for s...]
    unnamed x2 -> x0, blocking collectives: 54.7 us -> none
    psum x1, blocking collectives: 12.5 us -> 38.7 us  [body(): small = lax.psum(small, ('dp', 'tensor'))]
    unnamed x365 -> x79, local copies, waits for them, and re-layouts: 23.9 us -> 10.3 us
    reduce_sum x13 -> x2, other arithmetic: 14.1 us -> 3.21 us  [the longest x1 1.85 us: body(): jnp.sum(score1_low.astype(jnp.float32), axis=0)]
    dot_general x68 -> x24, matrix products: 48.8 us -> 38.9 us  [the longest x7 18.6 us: rows_dot_t(): lax.dot_general(rows, matrix, (((2,), (1,)), ((), ())), preferred_element...]
  transfers between devices with their start and end apart: 25 -> 0, of which waited for: 16 -> 0; matrix products, arithmetic and copies ran while one was open for 7% -> 0% of each run, Pallas kernels for 0% -> 0%
where the time goes in v1:
time: 355 us; the launch traced here: 353 us
  Pallas kernels  208 us (59%)
  matrix products  52.6 us (15%)
  local copies, waits for them, and re-layouts  42 us (12%)
  blocking collectives  38.7 us (11%)
  other arithmetic  10.5 us (3%)
    pallas_call x6, Pallas kernels, call(): pl.pallas_call(kernel, out_shape=[jax.ShapeDtypeStruct(shape, kind) for s...  208 us
    psum x1, blocking collectives, body(): small = lax.psum(small, ('dp', 'tensor'))  38.7 us
    dot_general x7, matrix products, rows_dot_t(): lax.dot_general(rows, matrix, (((2,), (1,)), ((), ())), preferred_element...  18.6 us
    dot_general x7, matrix products, rows_dot(): lax.dot_general(rows, matrix, (((2,), (0,)), ((), ())), preferred_element...  14.1 us
    dot_general x8, matrix products, dot_left_t(): lax.dot_general(left, right, (((0,), (0,)), ((), ())), preferred_element_...  10.4 us
    unnamed x79, local copies, waits for them, and re-layouts  10.3 us
    concatenate x1, local copies, waits for them, and re-layouts, body(): jnp.concatenate([weight_dot(normed3_all, gate_up_grad), weight_dot(cot_al...  7.54 us

profile of v1, /device:TPU:0, one launch (start us, length us, event | category | flops | bytes accessed | tf_op | source)
XLA Modules:
  0.0 353.4 jit_solution(16449712072679466603)
XLA Ops:
  11.4 2.8 reshape.175
  17.0 57.5 %entry_gather.1 = (bf16[8,96,3200]{2,1,0:T(8,128)(2,1)}, bf16[2,256,768]{2,1,0:T(8,128)(2,1)}, bf16[2,256,768]{2,1,0:T(8,128)(2,1)}, bf16[2,128,768]{2,1,0:T(8,128)(2,1)}) custom-call(bf16[96,3200]{1,0:T(8,128)(2,1)} %concatenate.27.refs_0_, bf16[2,64,768]{2,1,0:T(8,128)(2,1)} %refs_1_.3, bf16[2,64,768]{2,1,0:T(8,128)(2,1)} %grad_in.1, ...), custom_call_target="tpu_custom_call" | custom-call | tf_op jit(solution)/shard_map/entry_gather/pallas_call | solution.py:320
  80.8 2.0 convolution_convert_fusion.6
  82.8 2.0 fusion.48
  86.1 2.4 convolution_convert_fusion.5.parts
  88.5 30.7 %self_sum_norm.1 = (f32[2,64,768]{2,1,0:T(8,128)}, bf16[2,256,768]{2,1,0:T(8,128)(2,1)}) custom-call(bf16[2,256,768]{2,1,0:T(8,128)(2,1)} %convolution_convert_fusion.5.parts, bf16[2,64,768]{2,1,0:T(8,128)(2,1)} %refs_1_.3, f32[1,768]{1,0:T(1,128)} %get-tuple-element.173.gain), custom_call_target="tpu_custom_call" | custom-call | tf_op jit(solution)/shard_map/self_sum_norm/pallas_call | solution.py:320
  119.1 1.9 convolution_convert_fusion.12
  122.1 2.5 convolution_convert_fusion.4.parts
  124.6 30.4 %cross_sum_norm.1 = (f32[2,64,768]{2,1,0:T(8,128)}, bf16[2,256,768]{2,1,0:T(8,128)(2,1)}) custom-call(bf16[2,256,768]{2,1,0:T(8,128)(2,1)} %convolution_convert_fusion.4.parts, f32[2,64,768]{2,1,0:T(8,128)} %get-tuple-element.42.resid.values, f32[1,768]{1,0:T(1,128)} %get-tuple-element.172.gain), custom_call_target="tpu_custom_call" | custom-call | tf_op jit(solution)/shard_map/cross_sum_norm/pallas_call | solution.py:320
  155.1 2.7 fusion.13
  157.8 2.4 fusion.20
  161.7 2.7 convolution_convert_fusion.2.side_parts
  164.4 2.2 bitcast_convert_fusion
  166.6 3.3 convolution_convert_fusion.3.parts
  169.9 33.8 %feed_back.1 = (f32[2,64,768]{2,1,0:T(8,128)}, bf16[2,256,768]{2,1,0:T(8,128)(2,1)}, bf16[2,64,768]{2,1,0:T(8,128)(2,1)}, f32[1,768]{1,0:T(1,128)}) custom-call(bf16[2,256,768]{2,1,0:T(8,128)(2,1)} %convolution_convert_fusion.3.parts, bf16[2,256,768]{2,1,0:T(8,128)(2,1)} %convolution_convert_fusion.2.side_parts, ...), custom_call_target="tpu_custom_call" | custom-call | tf_op jit(solution)/shard_map/feed_back/pallas_call | solution.py:320
  214.6 2.2 convolution_convert_fusion.7.side_parts
  216.9 2.6 convolution_convert_fusion.1.parts
  219.4 29.7 %cross_back.1 = (f32[2,64,768]{2,1,0:T(8,128)}, bf16[2,256,768]{2,1,0:T(8,128)(2,1)}, f32[2,32,768]{2,1,0:T(8,128)}, f32[1,768]{1,0:T(1,128)}) custom-call(bf16[2,256,768]{2,1,0:T(8,128)(2,1)} %convolution_convert_fusion.1.parts, bf16[2,128,768]{2,1,0:T(8,128)(2,1)} %convolution_convert_fusion.7.side_parts, f32[2,64,768]{2,1,0:T(8,128)} %get-tuple-element.42.resid.values, ...), custom_call_target="tpu_custom_call" | custom-call | tf_op jit(solution)/shard_map/cross_back/pallas_call | solution.py:320
  259.2 3.0 convolution_convert_fusion.refs_0_
  265.6 7.5 %concatenate.32 = bf16[768,3072]{1,0:T(8,128)(2,1)} concatenate(bf16[768,1024]{1,0:T(8,128)(2,1)} %bitcast_convert_fusion, bf16[768,512]{1,0:T(8,128)(2,1)} %bitcast_convert_fusion.2, bf16[768,576]{1,0:T(8,128)(2,1)S(1)} %copy.209, bf16[768,192]{1,0:T(8,128)(2,1)S(1)} %copy-done.3, bf16[768,384]{1,0:T(8,128)(2,1)S(1)} %fusion.8, bf16[768,192]{1,0:T(8,128)(2,1)S(1)} %copy-done.4, ...), dimensions={1} | concatenate | bytes 9437184 | tf_op jit(solution)/shard_map/concatenate | solution.py:786
  273.1 26.3 %exit_sums.1 = (f32[2,64,768]{2,1,0:T(8,128)}, f32[1,768]{1,0:T(1,128)}, f32[96,3072]{1,0:T(8,128)}) custom-call(bf16[2,256,768]{2,1,0:T(8,128)(2,1)} %convolution_convert_fusion.refs_0_, bf16[2,64,768]{2,1,0:T(8,128)(2,1)} %refs_1_.3, f32[1,768]{1,0:T(1,128)} %get-tuple-element.170.refs_2_, f32[2,64,768]{2,1,0:T(8,128)} %get-tuple-element.49.refs_3_, ...), custom_call_target="tpu_custom_call" | custom-call | tf_op jit(solution)/shard_map/exit_sums/pallas_call | solution.py:320
  300.2 1.9 slice_bitcast_fusion.21
  306.1 3.4 reshape.184
  311.2 38.7 %psum.7 = f32[2688]{0:T(1024)S(1)} all-reduce(f32[2688]{0:T(1024)S(1)} %pad_maximum_fusion.9), channel_id=1, replica_groups=mesh['dp'=8,'tensor'=4] {'dp','tensor'}, use_global_device_ids=true, to_apply=%region_9.10 | all-reduce | flops 2688 | bytes 21504 | tf_op jit(solution)/shard_map/psum | solution.py:845
  (145 shorter events, 57.6 us)
Async XLA Ops:
  0.7 1.9 copy-start
  75.8 5.0 %copy-start.26 = (f32[2,256]{1,0:T(2,128)}, f32[2,256]{1,0:T(2,128)S(1)}, u32[]{:S(2)}) copy-start(f32[2,256]{1,0:T(2,128)S(1)} %add_rsqrt_fusion) | copy-start | bytes 6148
  75.8 5.0 %copy-start.7 = (bf16[2,256,768]{2,1,0:T(8,128)(2,1)S(1)}, bf16[2,256,768]{2,1,0:T(8,128)(2,1)}, u32[]{:S(2)}) copy-start(bf16[2,256,768]{2,1,0:T(8,128)(2,1)} %get-tuple-element.40) | copy-start | bytes 2359300
  80.8 2.0 copy-start.24
  82.8 2.0 copy-start.6
  82.8 2.0 copy-start.16
  84.8 170.2 %copy-start.5 = (f32[2,3,256,256]{2,3,1,0:T(8,128)}, f32[2,3,256,256]{2,3,1,0:T(8,128)S(1)}, u32[]{:S(2)}) copy-start(f32[2,3,256,256]{2,3,1,0:T(8,128)S(1)} %get-tuple-element.175) | copy-start | bytes 4718596
  86.1 35.0 %copy-start.15 = (bf16[2,128,192]{1,2,0:T(8,128)(2,1)S(1)}, bf16[2,128,192]{1,2,0:T(8,128)(2,1)}, u32[]{:S(2)}) copy-start(bf16[2,128,192]{1,2,0:T(8,128)(2,1)} %copy.193) | copy-start | bytes 294916
  86.1 35.0 %copy-start.21 = (pred[2,256,128]{1,2,0:T(8,128)(4,1)S(1)}, pred[2,256,128]{1,2,0:T(8,128)(4,1)}, u32[]{:S(2)}) copy-start(pred[2,256,128]{1,2,0:T(8,128)(4,1)} %broadcast_compare_fusion) | copy-start | bytes 196612
  119.1 2.4 copy-start.20
  121.0 86.6 %copy-start.11 = (bf16[2,256,192]{1,2,0:T(8,128)(2,1)}, bf16[2,256,192]{1,2,0:T(8,128)(2,1)S(1)}, u32[]{:S(2)}) copy-start(bf16[2,256,192]{1,2,0:T(8,128)(2,1)S(1)} %convolution_convert_fusion.12) | copy-start | bytes 589828
  155.0 2.7 copy-start.29
  161.7 2.7 copy-start.30
  216.9 33.0 %copy-start.10 = (bf16[2,3,64,256]{3,2,1,0:T(8,128)(2,1)S(1)}, bf16[2,3,64,256]{3,2,1,0:T(8,128)(2,1)}, u32[]{:S(2)}) copy-start(bf16[2,3,64,256]{3,2,1,0:T(8,128)(2,1)} %copy-done.9) | copy-start | bytes 589828
  249.9 4.1 %copy-start.23 = (f32[2,3,256]{2,1,0:T(4,128)S(1)}, f32[2,3,256]{2,1,0:T(4,128)}, u32[]{:S(2)}) copy-start(f32[2,3,256]{2,1,0:T(4,128)} %copy-done.22) | copy-start | bytes 18436
  259.2 3.0 copy-start.8
  259.2 3.0 copy-start.25
  259.2 3.0 copy-start.27
  263.9 1.6 copy-start.3
  263.9 1.6 copy-start.4
  299.4 2.7 copy-start.2
  309.9 41.4 %copy-start.18 = (bf16[2,64,768]{2,1,0:T(8,128)(2,1)S(1)}, bf16[2,64,768]{2,1,0:T(8,128)(2,1)}, u32[]{:S(2)}) copy-start(bf16[2,64,768]{2,1,0:T(8,128)(2,1)} %get-tuple-element.200) | copy-start | bytes 589828
  309.9 42.1 %copy-start.14 = (f32[2,64,768]{2,1,0:T(8,128)S(1)}, f32[2,64,768]{2,1,0:T(8,128)}, u32[]{:S(2)}) copy-start(f32[2,64,768]{2,1,0:T(8,128)} %get-tuple-element.201) | copy-start | bytes 1179652
  309.9 42.8 %copy-start.19 = (f32[2,32,768]{2,1,0:T(8,128)S(1)}, f32[2,32,768]{2,1,0:T(8,128)}, u32[]{:S(2)}) copy-start(f32[2,32,768]{2,1,0:T(8,128)} %get-tuple-element.202) | copy-start | bytes 589828
  (9 other events, 9.5 us)

commit v2 on v1

--- a/solution.py
+++ b/solution.py
@@ -27,16 +27,14 @@
 
 def greet(pos, count, cube_me):
     barrier = pltpu.get_barrier_semaphore()
-
-    @pl.when(pos > 0)
-    def _():
-        pl.semaphore_signal(barrier, inc=1, device_id={"tensor": pos - 1}, device_id_type=MESH)
-
-    @pl.when(pos < count - 1)
-    def _():
-        pl.semaphore_signal(barrier, inc=1, device_id={"tensor": pos + 1}, device_id_type=MESH)
-
-    waits = 2 - jnp.where(pos == 0, 1, 0) - jnp.where(pos == count - 1, 1, 0)
+    for away in range(1, count):
+        pl.semaphore_signal(
+            barrier,
+            inc=1,
+            device_id={"tensor": lax.rem(pos + away, count)},
+            device_id_type=MESH,
+        )
+    waits = count - 1
     if cube_me is not None:
         for flip in (1, 2, 4):
             pl.semaphore_signal(
@@ -44,6 +42,37 @@
             )
         waits = waits + 3
     pl.semaphore_wait(barrier, waits)
+
+
+def small_sum(pos, count, me, acc, cube_got, line_got, send, recv, line_send, line_recv):
+    for slot, flip in enumerate((1, 2, 4)):
+        one = pltpu.make_async_remote_copy(
+            src_ref=acc,
+            dst_ref=cube_got.at[slot],
+            send_sem=send.at[slot],
+            recv_sem=recv.at[slot],
+            device_id={"dp": me ^ flip},
+            device_id_type=MESH,
+        )
+        one.start()
+        one.wait()
+        acc[...] = acc[...] + cube_got[slot]
+    copies = []
+    for away in range(1, count):
+        one = pltpu.make_async_remote_copy(
+            src_ref=acc,
+            dst_ref=line_got.at[away - 1],
+            send_sem=line_send.at[away - 1],
+            recv_sem=line_recv.at[away - 1],
+            device_id={"tensor": lax.rem(pos + away, count)},
+            device_id_type=MESH,
+        )
+        one.start()
+        copies.append(one)
+    for one in copies:
+        one.wait()
+    for away in range(1, count):
+        acc[...] = acc[...] + line_got[away - 1]
 
 
 def line_gather(pos, count, buf, send, recv):
@@ -333,10 +362,10 @@
 def entry_kernel(count, with_cube, *refs):
     if with_cube:
         weights, refs = refs[0], refs[1:]
-    rows_in, refs = refs[:3], refs[3:]
+    rows_in, refs = refs[:2], refs[2:]
     if with_cube:
         weights_all, refs = refs[0], refs[1:]
-    rows_out, refs = refs[:3], refs[3:]
+    rows_out, refs = refs[:2], refs[2:]
     pos = lax.axis_index("tensor")
     me = lax.axis_index("dp") if with_cube else None
     for source, target in zip(rows_in, rows_out):
@@ -347,59 +376,65 @@
     greet(pos, count, me)
     streams = []
     if with_cube:
-        streams.append(cube_gather(me, weights_all, refs[6], refs[7]))
-
-    def lines():
-        for which in range(3):
-            yield from line_gather(
-                pos, count, rows_out[which], refs[2 * which], refs[2 * which + 1]
-            )
-
-    run_together(*streams, lines())
-
-
-def forward_kernel(
-    count, parts, resid, gain, total_out, normed_all, got, staged, s_send, s_recv, g_send, g_recv
-):
+        streams.append(cube_gather(me, weights_all, refs[4], refs[5]))
+    for which in range(2):
+        streams.append(
+            line_gather(pos, count, rows_out[which], refs[2 * which], refs[2 * which + 1])
+        )
+    run_together(*streams)
+
+
+def forward_kernel(count, beside, *refs):
+    parts, resid, gain = refs[:3]
+    refs = refs[3:]
+    if beside:
+        extra, refs = refs[0], refs[1:]
+    total_out, normed_all = refs[:2]
+    refs = refs[2:]
+    if beside:
+        extra_all, refs = refs[0], refs[1:]
+    got, staged, s_send, s_recv, g_send, g_recv = refs[:6]
     pos = lax.axis_index("tensor")
-    greet(pos, count, None)
-    run_together(line_scatter(pos, count, parts, got, staged, total_out, s_send, s_recv))
-    for step in range(parts.shape[0]):
-        total = total_out[step] + resid[step].astype(jnp.float32)
-        total_out[step] = total
-        normed_all[step, own_rows(pos, normed_all, count)] = norm_forward(total, gain[...]).astype(
-            jnp.bfloat16
-        )
-    run_together(line_gather(pos, count, normed_all, g_send, g_recv))
-
-
-def back_kernel(
-    count,
-    side_kind,
-    parts,
-    side_parts,
-    values,
-    gain,
-    grad_in,
-    side_resid,
-    grad_out,
-    gathered,
-    side_out,
-    gain_out,
-    got,
-    staged,
-    side_got,
-    side_staged,
-    side_total,
-    s_send,
-    s_recv,
-    t_send,
-    t_recv,
-    g_send,
-    g_recv,
-):
+    me = lax.axis_index("dp") if beside == "cube" else None
+    streams = []
+    if beside == "cube":
+        extra_all[me] = extra[...]
+    if beside == "line":
+        for step in range(extra.shape[0]):
+            extra_all[step, own_rows(pos, extra_all, count)] = extra[step]
+    greet(pos, count, me)
+
+    def main():
+        yield from line_scatter(pos, count, parts, got, staged, total_out, s_send, s_recv)
+        for step in range(parts.shape[0]):
+            total = total_out[step] + resid[step].astype(jnp.float32)
+            total_out[step] = total
+            normed_all[step, own_rows(pos, normed_all, count)] = norm_forward(
+                total, gain[...]
+            ).astype(jnp.bfloat16)
+        yield from line_gather(pos, count, normed_all, g_send, g_recv)
+
+    streams.append(main())
+    if beside == "cube":
+        streams.append(cube_gather(me, extra_all, refs[6], refs[7]))
+    if beside == "line":
+        streams.append(line_gather(pos, count, extra_all, refs[6], refs[7]))
+    run_together(*streams)
+
+
+def back_kernel(count, side_kind, cubes, *refs):
+    parts, side_parts, values, gain, grad_in, side_resid = refs[:6]
+    refs = refs[6:]
+    weight_parts, refs = refs[:cubes], refs[cubes:]
+    grad_out, gathered, side_out, gain_out = refs[:4]
+    refs = refs[4:]
+    weight_out, refs = refs[:cubes], refs[cubes:]
+    got, staged, side_got, side_staged, side_total = refs[:5]
+    s_send, s_recv, t_send, t_recv, g_send, g_recv = refs[5:11]
+    refs = refs[11:]
     pos = lax.axis_index("tensor")
-    greet(pos, count, None)
+    me = lax.axis_index("dp") if cubes else None
+    greet(pos, count, me)
 
     def main():
         yield from line_scatter(pos, count, parts, got, staged, grad_out, s_send, s_recv)
@@ -422,41 +457,63 @@
             else:
                 side_out[step] = side_total[step]
 
-    run_together(main(), side())
-
-
-def exit_kernel(count, with_cube, *refs):
-    parts, values, gain, grad_in = refs[:4]
-    refs = refs[4:]
-    if with_cube:
-        weight_parts, refs = refs[0], refs[1:]
-    grad_out, gain_out = refs[:2]
+    run_together(main(), side(), *cube_streams(me, weight_parts, weight_out, refs))
+
+
+def cube_streams(me, weight_parts, weight_out, refs):
+    return [
+        cube_scatter(
+            me,
+            weight_parts[which],
+            *refs[10 * which : 10 * which + 4],
+            weight_out[which],
+            *refs[10 * which + 4 : 10 * which + 10],
+        )
+        for which in range(len(weight_parts))
+    ]
+
+
+def cube_scratch(shard_rows, columns):
+    return [
+        pltpu.VMEM((4, shard_rows, columns), jnp.bfloat16),
+        pltpu.VMEM((4, shard_rows, columns), jnp.bfloat16),
+        pltpu.VMEM((2, 2, shard_rows // 2, columns), jnp.bfloat16),
+        pltpu.VMEM((2, shard_rows // 2, columns), jnp.bfloat16),
+        pltpu.SemaphoreType.DMA((4,)),
+        pltpu.SemaphoreType.DMA((4,)),
+        pltpu.SemaphoreType.DMA((2, 2)),
+        pltpu.SemaphoreType.DMA((2, 2)),
+        pltpu.SemaphoreType.DMA((2,)),
+        pltpu.SemaphoreType.DMA((2,)),
+    ]
+
+
+def exit_kernel(count, cubes, *refs):
+    parts, values, gain, grad_in, small = refs[:5]
+    refs = refs[5:]
+    weight_parts, refs = refs[:cubes], refs[cubes:]
+    grad_out, small_out = refs[:2]
     refs = refs[2:]
-    if with_cube:
-        weight_out, refs = refs[0], refs[1:]
+    weight_out, refs = refs[:cubes], refs[cubes:]
     got, staged, s_send, s_recv = refs[:4]
     refs = refs[4:]
     pos = lax.axis_index("tensor")
-    me = lax.axis_index("dp") if with_cube else None
+    me = lax.axis_index("dp") if cubes else None
     greet(pos, count, me)
 
     def main():
         yield from line_scatter(pos, count, parts, got, staged, grad_out, s_send, s_recv)
-        gain_out[...] = jnp.zeros_like(gain_out)
+        small_out[...] = small[...]
         for step in range(parts.shape[0]):
             moved, gain_part = norm_backward(
                 grad_out[step], values[step].astype(jnp.float32), gain[...]
             )
             grad_out[step] = grad_in[step] + moved
-            gain_out[...] = gain_out[...] + gain_part
-
-    streams = [main()]
-    if with_cube:
-        got1, sums, got2, got3 = refs[:4]
-        streams.insert(
-            0, cube_scatter(me, weight_parts, got1, sums, got2, got3, weight_out, *refs[4:])
-        )
-    run_together(*streams)
+            small_out[0:1] = small_out[0:1] + gain_part
+
+    run_together(main(), *cube_streams(me, weight_parts, weight_out, refs))
+    if cubes:
+        small_sum(pos, count, me, small_out, *refs[10 * cubes :])
 
 
 def dot_plain(left, right):
@@ -553,30 +610,40 @@
         left.reshape(-1, left.shape[-1]), right.reshape(-1, right.shape[-1])
     ).astype(jnp.bfloat16)
 
-def toeplitz_bias(bucket_low, table_local):
-    per_distance = jnp.dot(bucket_low, table_local, preferred_element_type=jnp.float32)
-    length = per_distance.shape[0]
-    reversed_rows = jnp.concatenate(
-        [per_distance[::-1].T, jnp.zeros((per_distance.shape[1], length), jnp.float32)], axis=1
-    )
-    tiled_rows = jnp.tile(reversed_rows, (1, length))
-    skewed = tiled_rows[:, : length * (2 * length - 1)].reshape(-1, length, 2 * length - 1)
-    return skewed[:, :, length - 1 :]
-
-
-def table_back(score_low, bucket_float):
-    heads_local = score_low.shape[0]
-    length = score_low.shape[1]
-    padded = jnp.concatenate(
-        [jnp.zeros((heads_local, length, length - 1), jnp.float32), score_low.astype(jnp.float32)],
-        axis=2,
-    )
-    flat_rows = jnp.concatenate(
-        [padded.reshape(heads_local, -1), jnp.zeros((heads_local, length), jnp.float32)], axis=1
-    )
-    folded = jnp.sum(flat_rows.reshape(heads_local, length, 2 * length), axis=1)
-    per_distance = folded[:, :length][:, ::-1].T
-    return dot_left_t(bucket_float, per_distance)
+def bias_kernel(rows, out):
+    length = out.shape[1]
+    for head in range(out.shape[0]):
+        out[head] = pltpu.roll(
+            jnp.broadcast_to(rows[head : head + 1], (length, length)), 0, 1, stride=1, stride_axis=0
+        )
+
+
+def diagonal_kernel(scores, out):
+    length = scores.shape[2]
+    turned = (
+        lax.broadcasted_iota(jnp.int32, (length, length), 0)
+        + lax.broadcasted_iota(jnp.int32, (length, length), 1)
+        == length - 1
+    ).astype(jnp.bfloat16)
+    for head in range(scores.shape[1]):
+        flipped = jnp.dot(turned, scores[0, head], preferred_element_type=jnp.float32)
+        for step in range(1, scores.shape[0]):
+            flipped = flipped + jnp.dot(
+                turned, scores[step, head], preferred_element_type=jnp.float32
+            )
+        moved = pltpu.roll(flipped, 1, 1, stride=1, stride_axis=0)
+        out[head : head + 1] = jnp.sum(moved, axis=0, keepdims=True)
+
+
+def local_call(kernel, shape, name, arg):
+    return pl.pallas_call(
+        kernel,
+        out_shape=jax.ShapeDtypeStruct(shape, jnp.float32),
+        in_specs=[pl.BlockSpec(memory_space=pltpu.VMEM)],
+        out_specs=pl.BlockSpec(memory_space=pltpu.VMEM),
+        compiler_params=pltpu.CompilerParams(vmem_limit_bytes=VMEM_LIMIT),
+        name=name,
+    )(arg)
 
 
 def body(
@@ -620,9 +687,6 @@
     )
     packed = jnp.concatenate(
         [
-            gate_weight,
-            up_weight,
-            down_weight.T,
             self_query,
             self_key,
             self_value,
@@ -635,20 +699,19 @@
         ],
         axis=1,
     )
+    packed_feed = jnp.concatenate([gate_weight, up_weight, down_weight.T], axis=1)
+    cube_sems = [pltpu.SemaphoreType.DMA((8, 2)), pltpu.SemaphoreType.DMA((CUBE, 2))]
     rows_shape = (micro, seq_len, width)
     enc_shape = (micro, enc_len, width)
     own_shape = (micro, row_count, width)
     line_sems = gather_sems(count, micro)
-    entry_args = [tokens, cotangent, encoder]
-    entry_outs = [(rows_shape, low), (rows_shape, low), (enc_shape, low)]
-    entry_scratch = line_sems * 3
+    entry_args = [tokens, encoder]
+    entry_outs = [(rows_shape, low), (enc_shape, low)]
+    entry_scratch = line_sems * 2
     if with_cube:
         entry_args.insert(0, packed)
         entry_outs.insert(0, ((CUBE,) + packed.shape, low))
-        entry_scratch = entry_scratch + [
-            pltpu.SemaphoreType.DMA((8, 2)),
-            pltpu.SemaphoreType.DMA((CUBE, 2)),
-        ]
+        entry_scratch = entry_scratch + cube_sems
     entry = call(
         functools.partial(entry_kernel, count, with_cube),
         entry_outs,
@@ -658,14 +721,12 @@
         *entry_args,
     )
     if with_cube:
-        whole, tokens_all, cot_all, encoder_all = entry
+        whole, tokens_all, encoder_all = entry
         whole = whole.reshape(width, packed.shape[1])
     else:
-        tokens_all, cot_all, encoder_all = entry
+        tokens_all, encoder_all = entry
         whole = lax.all_gather(packed, "dp", axis=0, tiled=True)
-    w_gate_up = whole[:, : 2 * hidden_local]
-    w_down_t = whole[:, 2 * hidden_local : 3 * hidden_local]
-    base = 3 * hidden_local
+    base = 0
     w_qkv = whole[:, base : base + 3 * inner]
     w_cq = whole[:, base + 3 * inner : base + 4 * inner]
     w_ckv = whole[:, base + 4 * inner : base + 6 * inner]
@@ -676,8 +737,14 @@
 
     position = jnp.arange(seq_len, dtype=jnp.int32)
     causal = position[:, None] >= position[None, :]
-    bucket_hits = buckets[:, None] == jnp.arange(BUCKETS, dtype=jnp.int32)[None, :]
-    bias_full = toeplitz_bias(bucket_hits.astype(low), bias_table)
+    buckets_back = jnp.concatenate([buckets[:1], buckets[1:][::-1]])
+    hits_back = buckets_back[:, None] == jnp.arange(BUCKETS, dtype=jnp.int32)[None, :]
+    bias_rows = lax.dot_general(
+        bias_table, hits_back.astype(low), (((0,), (1,)), ((), ())), preferred_element_type=jnp.float32
+    )
+    bias_full = local_call(
+        bias_kernel, (heads_local, seq_len, seq_len), "bias_spread", bias_rows
+    )
     dec_seg = dec_segments[:, 0]
     enc_seg = enc_segments[:, 0]
     self_allowed = causal[None] & (dec_seg[:, :, None] == dec_seg[:, None, :])
@@ -694,29 +761,41 @@
         qkv[..., 2 * inner :],
     )
     mixed1, probs1 = attend_forward(query1, key1, value1, heads_local, bias_full, self_allowed)
-    first, normed2_all = call(
-        functools.partial(forward_kernel, count),
-        [(own_shape, jnp.float32), (rows_shape, low)],
-        forward_scratch,
+    self_args = [rows_dot_t(mixed1, w_so_t).astype(low), tokens, gain2]
+    self_outs = [(own_shape, jnp.float32), (rows_shape, low)]
+    if with_cube:
+        self_args.append(packed_feed)
+        self_outs.append(((CUBE,) + packed_feed.shape, low))
+    self_ended = call(
+        functools.partial(forward_kernel, count, "cube" if with_cube else ""),
+        self_outs,
+        forward_scratch + (cube_sems if with_cube else []),
         1,
         "self_sum_norm",
-        rows_dot_t(mixed1, w_so_t).astype(low),
-        tokens,
-        gain2,
-    )
+        *self_args,
+    )
+    if with_cube:
+        first, normed2_all, feed_whole = self_ended
+        feed_whole = feed_whole.reshape(width, packed_feed.shape[1])
+    else:
+        first, normed2_all = self_ended
+        feed_whole = lax.all_gather(packed_feed, "dp", axis=0, tiled=True)
+    w_gate_up = feed_whole[:, : 2 * hidden_local]
+    w_down_t = feed_whole[:, 2 * hidden_local :]
     key_value2 = rows_dot(encoder_all, w_ckv).astype(low)
     key2, value2 = key_value2[..., :inner], key_value2[..., inner:]
     query2 = rows_dot(normed2_all, w_cq).astype(low)
     mixed2, probs2 = attend_forward(query2, key2, value2, heads_local, 0.0, cross_allowed)
-    second, normed3_all = call(
-        functools.partial(forward_kernel, count),
-        [(own_shape, jnp.float32), (rows_shape, low)],
-        forward_scratch,
+    second, normed3_all, cot_all = call(
+        functools.partial(forward_kernel, count, "line"),
+        [(own_shape, jnp.float32), (rows_shape, low), (rows_shape, low)],
+        forward_scratch + gather_sems(count, micro),
         2,
         "cross_sum_norm",
         rows_dot_t(mixed2, w_co_t).astype(low),
         first,
         gain3,
+        cotangent,
     )
     gate_up = rows_dot(normed3_all, w_gate_up)
     gate_pre, up_pre = gate_up[..., :hidden_local], gate_up[..., hidden_local:]
@@ -737,7 +816,7 @@
         )
 
     second_grad, cross_out_all, layer_out, gain3_part = call(
-        functools.partial(back_kernel, count, "out"),
+        functools.partial(back_kernel, count, "out", 0),
         [
             (own_shape, jnp.float32),
             (rows_shape, low),
@@ -760,15 +839,42 @@
     )
     key_value2_grad = jnp.concatenate([key2_grad, value2_grad], axis=-1)
     enc_own = (micro, encoder.shape[1], width)
-    first_grad, self_out_all, encoder_grad, gain2_part = call(
-        functools.partial(back_kernel, count, "plain"),
+    feed_parts = [
+        weight_dot(normed3_all, gate_up_grad),
+        weight_dot(cot_all, hidden),
+    ]
+
+    def cube_args(parts):
+        return [one.reshape(CUBE, shard_rows, one.shape[1]) for one in parts] if with_cube else []
+
+    def cube_outs(parts):
+        return [((shard_rows, one.shape[1]), jnp.float32) for one in parts] if with_cube else []
+
+    def cube_space(parts):
+        scratch = []
+        if with_cube:
+            for one in parts:
+                scratch = scratch + cube_scratch(shard_rows, one.shape[1])
+        return scratch
+
+    def owned_parts(ended, parts):
+        if with_cube:
+            return ended
+        return [
+            lax.psum_scatter(one.astype(jnp.float32), "dp", scatter_dimension=0, tiled=True)
+            for one in parts
+        ]
+
+    first_grad, self_out_all, encoder_grad, gain2_part, *feed_ended = call(
+        functools.partial(back_kernel, count, "plain", len(cube_args(feed_parts))),
         [
             (own_shape, jnp.float32),
             (rows_shape, low),
             (enc_own, jnp.float32),
             ((1, width), jnp.float32),
-        ],
-        back_scratch(enc_shape, enc_own),
+        ]
+        + cube_outs(feed_parts),
+        back_scratch(enc_shape, enc_own) + cube_space(feed_parts),
         4,
         "cross_back",
         rows_dot_t(query2_grad, w_cq).astype(low),
@@ -777,100 +883,104 @@
         gain2,
         second_grad,
         second,
+        *cube_args(feed_parts),
     )
     mixed1_grad = rows_dot(self_out_all, w_so_t).astype(low)
     query1_grad, key1_grad, value1_grad, score1_low = attend_backward(
         query1, key1, value1, heads_local, probs1, mixed1_grad
     )
     qkv_grad = jnp.concatenate([query1_grad, key1_grad, value1_grad], axis=-1)
-    weight_parts = jnp.concatenate(
+    head_parts = [
+        weight_dot(normed1_all, qkv_grad),
+        jnp.concatenate(
+            [
+                weight_dot(normed2_all, query2_grad),
+                weight_dot(encoder_all, key_value2_grad),
+                weight_dot(self_out_all, mixed1),
+                weight_dot(cross_out_all, mixed2),
+            ],
+            axis=1,
+        ),
+    ]
+    per_distance = local_call(
+        diagonal_kernel, (heads_local, seq_len), "diagonal_sums", score1_low
+    )
+    tables = lax.dot_general(
+        hits_back.astype(jnp.float32),
+        per_distance,
+        (((0,), (1,)), ((), ())),
+        precision=lax.Precision.HIGHEST,
+        preferred_element_type=jnp.float32,
+    )
+    pos = lax.axis_index("tensor")
+    table_size = tables.shape[0] * tables.shape[1]
+    placed_table = jnp.where(
+        (jnp.arange(count, dtype=jnp.int32) == pos)[:, None], tables.reshape(1, -1), 0.0
+    ).reshape(1, -1)
+    small = jnp.concatenate(
         [
-            weight_dot(normed3_all, gate_up_grad),
-            weight_dot(cot_all, hidden),
-            weight_dot(normed1_all, qkv_grad),
-            weight_dot(normed2_all, query2_grad),
-            weight_dot(encoder_all, key_value2_grad),
-            weight_dot(self_out_all, mixed1),
-            weight_dot(cross_out_all, mixed2),
+            jnp.zeros((1, width), jnp.float32),
+            gain2_part,
+            gain3_part,
+            jnp.pad(placed_table, ((0, 0), (0, width - count * table_size))),
+            jnp.zeros((4, width), jnp.float32),
         ],
-        axis=1,
-    )
-    columns = weight_parts.shape[1]
-    exit_args = [rows_dot_t(qkv_grad, w_qkv).astype(low), tokens, gain1, first_grad]
-    exit_outs = [(own_shape, jnp.float32), ((1, width), jnp.float32)]
-    exit_scratch = scatter_scratch(rows_shape) + scatter_sems(count, micro)
+        axis=0,
+    )
+    exit_scratch = (
+        scatter_scratch(rows_shape) + scatter_sems(count, micro) + cube_space(head_parts)
+    )
     if with_cube:
-        exit_args.append(weight_parts.reshape(CUBE, shard_rows, columns))
-        exit_outs.append(((shard_rows, columns), jnp.float32))
         exit_scratch = exit_scratch + [
-            pltpu.VMEM((4, shard_rows, columns), low),
-            pltpu.VMEM((4, shard_rows, columns), low),
-            pltpu.VMEM((2, 2, shard_rows // 2, columns), low),
-            pltpu.VMEM((2, shard_rows // 2, columns), low),
-            pltpu.SemaphoreType.DMA((4,)),
-            pltpu.SemaphoreType.DMA((4,)),
-            pltpu.SemaphoreType.DMA((2, 2)),
-            pltpu.SemaphoreType.DMA((2, 2)),
-            pltpu.SemaphoreType.DMA((2,)),
-            pltpu.SemaphoreType.DMA((2,)),
+            pltpu.VMEM((3,) + small.shape, jnp.float32),
+            pltpu.VMEM((count - 1,) + small.shape, jnp.float32),
+            pltpu.SemaphoreType.DMA((3,)),
+            pltpu.SemaphoreType.DMA((3,)),
+            pltpu.SemaphoreType.DMA((count - 1,)),
+            pltpu.SemaphoreType.DMA((count - 1,)),
         ]
-    ended = call(
-        functools.partial(exit_kernel, count, with_cube),
-        exit_outs,
+    token_grad, small_out, *head_ended = call(
+        functools.partial(exit_kernel, count, len(cube_args(head_parts))),
+        [(own_shape, jnp.float32), (small.shape, jnp.float32)] + cube_outs(head_parts),
         exit_scratch,
         5,
         "exit_sums",
-        *exit_args,
-    )
-    if with_cube:
-        token_grad, gain1_part, owned = ended
-    else:
-        token_grad, gain1_part = ended
-        owned = lax.psum_scatter(
-            weight_parts.astype(jnp.float32), "dp", scatter_dimension=0, tiled=True
-        )
-    tables = table_back(jnp.sum(score1_low.astype(jnp.float32), axis=0), bucket_hits.astype(jnp.float32))
-    pos = lax.axis_index("tensor")
-    placed_table = jnp.where(
-        (jnp.arange(count, dtype=jnp.int32) == pos)[:, None, None], tables[None], 0.0
-    )
-    small = jnp.concatenate(
-        [
-            gain1_part.reshape(-1),
-            gain2_part.reshape(-1),
-            gain3_part.reshape(-1),
-            placed_table.reshape(-1),
-        ]
-    )
-    small = lax.psum(small, ("dp", "tensor"))
+        rows_dot_t(qkv_grad, w_qkv).astype(low),
+        tokens,
+        gain1,
+        first_grad,
+        small,
+        *cube_args(head_parts),
+    )
+    if not with_cube:
+        small_out = lax.psum(small_out, ("dp", "tensor"))
+    gate_up_owned, down_owned = owned_parts(feed_ended, feed_parts)
+    qkv_owned, others = owned_parts(head_ended, head_parts)
     index = lax.axis_index("dp") * count + pos
     piece = width // (dp_count * count)
     gain_grads = tuple(
-        lax.dynamic_slice(small, (which * width + index * piece,), (piece,)) for which in range(3)
-    )
-    table_size = tables.shape[0] * tables.shape[1]
-    table_grad = lax.dynamic_slice(small, (3 * width + pos * table_size,), (table_size,)).reshape(
+        lax.dynamic_slice(small_out, (which, index * piece), (1, piece)).reshape(-1)
+        for which in range(3)
+    )
+    table_grad = lax.dynamic_slice(small_out, (3, pos * table_size), (1, table_size)).reshape(
         tables.shape
     )
-
-    def wide(start, size):
-        return owned[:, start : start + size]
 
     return (
         layer_out,
         token_grad,
         encoder_grad,
-        wide(base, inner),
-        wide(base + inner, inner),
-        wide(base + 2 * inner, inner),
-        wide(base + 6 * inner, inner).T,
-        wide(base + 3 * inner, inner),
-        wide(base + 4 * inner, inner),
-        wide(base + 5 * inner, inner),
-        wide(base + 7 * inner, inner).T,
-        wide(0, hidden_local),
-        wide(hidden_local, hidden_local),
-        wide(2 * hidden_local, hidden_local).T,
+        qkv_owned[:, :inner],
+        qkv_owned[:, inner : 2 * inner],
+        qkv_owned[:, 2 * inner :],
+        others[:, 3 * inner : 4 * inner].T,
+        others[:, :inner],
+        others[:, inner : 2 * inner],
+        others[:, 2 * inner : 3 * inner],
+        others[:, 4 * inner :].T,
+        gate_up_owned[:, :hidden_local],
+        gate_up_owned[:, hidden_local:],
+        down_owned.T,
     ) + gain_grads + (table_grad,)
 
 

time: 355 us -> 302 us (0.85)
  blocking collectives: 38.7 us -> 0 us
  local copies, waits for them, and re-layouts: 42 us -> 24.8 us
  Pallas kernels: 208 us -> 216 us
    psum x1 -> x0, blocking collectives: 38.7 us -> none  [body(): small = lax.psum(small, ('dp', 'tensor'))]
    concatenate x5 -> x3, local copies, waits for them, and re-layouts: 11.4 us -> 4.07 us  [the longest x1 1.81 us: body(): jnp.concatenate([self_query, self_key, self_value, cross_query, cross_key...]
    dot_general x7, matrix products: 18.6 us -> 11.7 us  [rows_dot_t(): lax.dot_general(rows, matrix, (((2,), (1,)), ((), ())), preferred_element...]
    reshape x3 -> x2, local copies, waits for them, and re-layouts: 6.35 us -> 1.49 us  [the longest x1 1.4 us: body(): lax.dynamic_slice(small_out, (which, index * piece), (1, piece)).reshape(-1)]
    pallas_call x0 -> x2, Pallas kernels: none -> 4.02 us  [local_call(): pl.pallas_call(kernel, out_shape=jax.ShapeDtypeStruct(shape, jnp.float32)...]
    unnamed x79 -> x111, local copies, waits for them, and re-layouts: 10.3 us -> 8.34 us
    dot_general x8 -> x7, matrix products: 10.4 us -> 9.5 us  [dot_left_t(): lax.dot_general(left, right, (((0,), (0,)), ((), ())), preferred_element_...]
where the time goes in v2:
time: 302 us; the launch traced here: 301 us
  Pallas kernels  216 us (72%)
  matrix products  51.8 us (17%)
  local copies, waits for them, and re-layouts  24.8 us (8%)
  other arithmetic  7.39 us (2%)
    pallas_call x6, Pallas kernels, call(): pl.pallas_call(kernel, out_shape=[jax.ShapeDtypeStruct(shape, kind) for s...  212 us
    dot_general x7, matrix products, rows_dot_t(): lax.dot_general(rows, matrix, (((2,), (1,)), ((), ())), preferred_element...  11.7 us
    dot_general x7, matrix products, rows_dot(): lax.dot_general(rows, matrix, (((2,), (0,)), ((), ())), preferred_element...  10.6 us
    dot_general x7, matrix products, dot_left_t(): lax.dot_general(left, right, (((0,), (0,)), ((), ())), preferred_element_...  9.5 us
    unnamed x111, local copies, waits for them, and re-layouts  8.34 us

profile of v2, /device:TPU:0, one launch (start us, length us, event | category | flops | bytes accessed | tf_op | source)
XLA Modules:
  0.0 301.1 jit_solution(9292184540468762760)
XLA Ops:
  3.3 1.8 concatenate.24.refs_0_
  5.1 28.8 %entry_gather.1 = (bf16[8,96,1664]{2,1,0:T(8,128)(2,1)}, bf16[2,256,768]{2,1,0:T(8,128)(2,1)}, bf16[2,128,768]{2,1,0:T(8,128)(2,1)}) custom-call(bf16[96,1664]{1,0:T(8,128)(2,1)} %concatenate.24.refs_0_, bf16[2,64,768]{2,1,0:T(8,128)(2,1)} %refs_1_.5, bf16[2,32,768]{2,1,0:T(8,128)(2,1)} %refs_2_.1), custom_call_target="tpu_custom_call" | custom-call | tf_op jit(solution)/shard_map/entry_gather/pallas_call | solution.py:349
  37.1 2.0 convolution_convert_fusion.6
  41.5 1.8 bias_spread.1
  43.5 3.1 %fusion.48 = (f32[2,3,256]{2,1,0:T(4,128)S(1)}, f32[2,3,256,256]{3,2,1,0:T(8,128)}) fusion(bf16[2,256,3,64]{1,3,2,0:T(8,128)(2,1)S(1)} %bitcast.194, bf16[2,256,3,64]{1,3,2,0:T(8,128)(2,1)S(1)} %bitcast.190, f32[3,256,256]{2,1,0:T(8,128)} %bias_spread.1, pred[2,256,256]{2,1,0:T(8,128)(4,1)S(1)} %compare_and_fusion), kind=kOutput, calls=%fused_computation.118 | convolution fusion | flops 51904768 | bytes 2889728 | tf_op jit(solution)/shard_map/sub | solution.py:555
  46.6 2.3 convolution_convert_fusion.16
  50.2 1.8 pad_maximum_fusion.5.refs_3_
  51.9 33.7 %self_sum_norm.1 = (f32[2,64,768]{2,1,0:T(8,128)}, bf16[2,256,768]{2,1,0:T(8,128)(2,1)}, bf16[8,96,1536]{2,1,0:T(8,128)(2,1)}) custom-call(bf16[2,256,768]{2,1,0:T(8,128)(2,1)} %convolution_convert_fusion.5.refs_0_, bf16[2,64,768]{2,1,0:T(8,128)(2,1)} %refs_1_.5, f32[1,768]{1,0:T(1,128)} %get-tuple-element.142.refs_2_.refs_3_, ...), custom_call_target="tpu_custom_call" | custom-call | tf_op jit(solution)/shard_map/self_sum_norm/pallas_call | solution.py:349
  89.4 2.9 fusion.49
  95.3 36.8 %cross_sum_norm.1 = (f32[2,64,768]{2,1,0:T(8,128)}, bf16[2,256,768]{2,1,0:T(8,128)(2,1)}, bf16[2,256,768]{2,1,0:T(8,128)(2,1)}) custom-call(bf16[2,256,768]{2,1,0:T(8,128)(2,1)} %convolution_convert_fusion.4.refs_0_, f32[2,64,768]{2,1,0:T(8,128)} %get-tuple-element.45.refs_1_.refs_2_, f32[1,768]{1,0:T(1,128)} %get-tuple-element.141.refs_2_.refs_3_, ...), custom_call_target="tpu_custom_call" | custom-call | tf_op jit(solution)/shard_map/cross_sum_norm/pallas_call | solution.py:349
  132.1 2.2 fusion.13
  137.1 1.9 convolution_convert_fusion.3.refs_0_
  139.0 39.5 %feed_back.1 = (f32[2,64,768]{2,1,0:T(8,128)}, bf16[2,256,768]{2,1,0:T(8,128)(2,1)}, bf16[2,64,768]{2,1,0:T(8,128)(2,1)}, f32[1,768]{1,0:T(1,128)}) custom-call(bf16[2,256,768]{2,1,0:T(8,128)(2,1)} %convolution_convert_fusion.3.refs_0_, bf16[2,256,768]{2,1,0:T(8,128)(2,1)} %convolution_convert_fusion.2.refs_1_, ...), custom_call_target="tpu_custom_call" | custom-call | tf_op jit(solution)/shard_map/feed_back/pallas_call | solution.py:349
  178.6 1.7 convolution_convert_fusion.10
  185.0 2.2 convolution_convert_fusion.18
  190.5 2.8 bitcast_convert_fusion.2
  193.4 2.1 bitcast_convert_fusion
  198.2 39.8 %cross_back.1 = (f32[2,64,768]{2,1,0:T(8,128)}, bf16[2,256,768]{2,1,0:T(8,128)(2,1)}, f32[2,32,768]{2,1,0:T(8,128)}, f32[1,768]{1,0:T(1,128)}, f32[96,1024]{1,0:T(8,128)}, /*index=5*/f32[96,512]{1,0:T(8,128)}) custom-call(bf16[2,256,768]{2,1,0:T(8,128)(2,1)} %convolution_convert_fusion.1.refs_0_, bf16[2,128,768]{2,1,0:T(8,128)(2,1)} %convolution_convert_fusion.7.refs_1_, ...), custom_call_target="tpu_custom_call" | custom-call | tf_op jit(solution)/shard_map/cross_back/pallas_call | solution.py:349
  243.0 2.2 multiply_reduce_fusion
  246.4 2.2 convolution_convert_fusion.13
  250.8 2.2 diagonal_sums.1
  255.0 2.9 convolution_convert_fusion.refs_0_
  257.9 32.9 %exit_sums.1 = (f32[2,64,768]{2,1,0:T(8,128)}, f32[8,768]{1,0:T(8,128)}, f32[96,576]{1,0:T(8,128)}, f32[96,960]{1,0:T(8,128)}) custom-call(bf16[2,256,768]{2,1,0:T(8,128)(2,1)} %convolution_convert_fusion.refs_0_, bf16[2,64,768]{2,1,0:T(8,128)(2,1)} %refs_1_.5, f32[1,768]{1,0:T(1,128)} %get-tuple-element.139.refs_2_, ...), custom_call_target="tpu_custom_call" | custom-call | tf_op jit(solution)/shard_map/exit_sums/pallas_call | solution.py:349
  290.9 2.2 slice_bitcast_fusion.21
  (169 shorter events, 47.8 us)
Async XLA Ops:
  0.7 40.0 %copy-start = (bf16[32,3]{0,1:T(4,128)(2,1)S(1)}, bf16[32,3]{0,1:T(4,128)(2,1)}, u32[]{:S(2)}) copy-start(bf16[32,3]{0,1:T(4,128)(2,1)} %param.41) | copy-start | bytes 580
  39.2 7.4 %copy-start.22 = (bf16[2,256,192]{1,2,0:T(8,128)(2,1)}, bf16[2,256,192]{1,2,0:T(8,128)(2,1)S(1)}, u32[]{:S(2)}) copy-start(bf16[2,256,192]{1,2,0:T(8,128)(2,1)S(1)} %get-tuple-element.123) | copy-start | bytes 589828
  40.7 5.9 %copy-start.39 = (s32[256]{0:T(256)}, s32[256]{0:T(256)S(1)}, u32[]{:S(2)}) copy-start(s32[256]{0:T(256)S(1)} %pad_add_fusion) | copy-start | bytes 3076
  43.5 5.4 %copy-start.28 = (pred[2,256,256]{2,1,0:T(8,128)(4,1)}, pred[2,256,256]{2,1,0:T(8,128)(4,1)S(1)}, u32[]{:S(2)}) copy-start(pred[2,256,256]{2,1,0:T(8,128)(4,1)S(1)} %compare_and_fusion) | copy-start | bytes 393220
  48.8 36.8 %copy-start.10 = (bf16[2,3,64,256]{3,2,1,0:T(8,128)(2,1)}, bf16[2,3,64,256]{3,2,1,0:T(8,128)(2,1)S(1)}, u32[]{:S(2)}) copy-start(bf16[2,3,64,256]{3,2,1,0:T(8,128)(2,1)S(1)} %convolution_convert_fusion.16) | copy-start | bytes 589828
  50.2 37.2 %copy-start.18 = (bf16[2,128,768]{2,1,0:T(8,128)(2,1)S(1)}, bf16[2,128,768]{2,1,0:T(8,128)(2,1)}, u32[]{:S(2)}) copy-start(bf16[2,128,768]{2,1,0:T(8,128)(2,1)} %get-tuple-element.41) | copy-start | bytes 1179652
  87.3 44.8 %copy-start.14 = (bf16[2,256,192]{1,2,0:T(8,128)(2,1)}, bf16[2,256,192]{1,2,0:T(8,128)(2,1)S(1)}, u32[]{:S(2)}) copy-start(bf16[2,256,192]{1,2,0:T(8,128)(2,1)S(1)} %convolution_convert_fusion.12) | copy-start | bytes 589828
  93.8 40.5 %copy-start.12 = (bf16[2,3,64,256]{3,2,1,0:T(8,128)(2,1)}, bf16[2,3,64,256]{3,2,1,0:T(8,128)(2,1)S(1)}, u32[]{:S(2)}) copy-start(bf16[2,3,64,256]{3,2,1,0:T(8,128)(2,1)S(1)} %convolution_convert_fusion.11) | copy-start | bytes 589828
  93.8 38.3 %copy-start.41 = (bf16[8,96,1536]{2,1,0:T(8,128)(2,1)S(1)}, bf16[8,96,1536]{2,1,0:T(8,128)(2,1)}, u32[]{:S(2)}) copy-start(bf16[8,96,1536]{2,1,0:T(8,128)(2,1)} %get-tuple-element.47) | copy-start | bytes 7077892
  139.0 41.3 %copy-start.9 = (f32[2,3,256,128]{2,3,1,0:T(8,128)S(1)}, f32[2,3,256,128]{2,3,1,0:T(8,128)}, u32[]{:S(2)}) copy-start(f32[2,3,256,128]{2,3,1,0:T(8,128)} %get-tuple-element.146) | copy-start | bytes 2359300
  139.0 41.3 %copy-start.30 = (f32[2,3,256]{2,1,0:T(4,128)S(1)}, f32[2,3,256]{2,1,0:T(4,128)}, u32[]{:S(2)}) copy-start(f32[2,3,256]{2,1,0:T(4,128)} %get-tuple-element.145) | copy-start | bytes 18436
  188.9 4.5 %copy-start.42 = (bf16[2,256,768]{2,1,0:T(8,128)(2,1)S(1)}, bf16[2,256,768]{2,1,0:T(8,128)(2,1)}, u32[]{:S(2)}) copy-start(bf16[2,256,768]{2,1,0:T(8,128)(2,1)} %get-tuple-element.48) | copy-start | bytes 2359300
  188.9 4.5 %copy-start.46 = (bf16[2,256,512]{2,1,0:T(8,128)(2,1)S(1)}, bf16[2,256,512]{2,1,0:T(8,128)(2,1)}, u32[]{:S(2)}) copy-start(bf16[2,256,512]{2,1,0:T(8,128)(2,1)} %copy-done.45) | copy-start | bytes 1572868
  188.9 4.5 %copy-start.48 = (bf16[2,256,512]{2,1,0:T(8,128)(2,1)S(1)}, bf16[2,256,512]{2,1,0:T(8,128)(2,1)}, u32[]{:S(2)}) copy-start(bf16[2,256,512]{2,1,0:T(8,128)(2,1)} %copy-done.47) | copy-start | bytes 1572868
  198.2 39.9 %copy-start.11 = (bf16[2,3,64,256]{3,2,1,0:T(8,128)(2,1)S(1)}, bf16[2,3,64,256]{3,2,1,0:T(8,128)(2,1)}, u32[]{:S(2)}) copy-start(bf16[2,3,64,256]{3,2,1,0:T(8,128)(2,1)} %copy-done.10) | copy-start | bytes 589828
  198.2 41.3 %copy-start.2 = (bf16[2,256,768]{2,1,0:T(8,128)(2,1)S(1)}, bf16[2,256,768]{2,1,0:T(8,128)(2,1)}, u32[]{:S(2)}) copy-start(bf16[2,256,768]{2,1,0:T(8,128)(2,1)} %get-tuple-element.51) | copy-start | bytes 2359300
  198.2 41.3 %copy-start.13 = (bf16[2,3,64,256]{3,2,1,0:T(8,128)(2,1)S(1)}, bf16[2,3,64,256]{3,2,1,0:T(8,128)(2,1)}, u32[]{:S(2)}) copy-start(bf16[2,3,64,256]{3,2,1,0:T(8,128)(2,1)} %copy-done.12) | copy-start | bytes 589828
  249.5 4.9 %copy-start.33 = (f32[1,768]{1,0:T(1,128)S(1)}, f32[1,768]{1,0:T(1,128)}, u32[]{:S(2)}) copy-start(f32[1,768]{1,0:T(1,128)} %get-tuple-element.56) | copy-start | bytes 9220
  249.5 4.9 %copy-start.34 = (f32[1,768]{1,0:T(1,128)S(1)}, f32[1,768]{1,0:T(1,128)}, u32[]{:S(2)}) copy-start(f32[1,768]{1,0:T(1,128)} %get-tuple-element.55) | copy-start | bytes 9220
  290.8 6.7 %copy-start.19 = (f32[96,1024]{1,0:T(8,128)S(1)}, f32[96,1024]{1,0:T(8,128)}, u32[]{:S(2)}) copy-start(f32[96,1024]{1,0:T(8,128)} %get-tuple-element.61) | copy-start | bytes 1179652
  290.8 7.4 %copy-start.24 = (bf16[2,64,768]{2,1,0:T(8,128)(2,1)S(1)}, bf16[2,64,768]{2,1,0:T(8,128)(2,1)}, u32[]{:S(2)}) copy-start(bf16[2,64,768]{2,1,0:T(8,128)(2,1)} %get-tuple-element.172) | copy-start | bytes 589828
  290.9 8.1 %copy-start.20 = (f32[2,64,768]{2,1,0:T(8,128)S(1)}, f32[2,64,768]{2,1,0:T(8,128)}, u32[]{:S(2)}) copy-start(f32[2,64,768]{2,1,0:T(8,128)} %get-tuple-element.173) | copy-start | bytes 1179652
  293.1 6.6 %copy-start.26 = (f32[2,32,768]{2,1,0:T(8,128)S(1)}, f32[2,32,768]{2,1,0:T(8,128)}, u32[]{:S(2)}) copy-start(f32[2,32,768]{2,1,0:T(8,128)} %get-tuple-element.174) | copy-start | bytes 589828
  293.1 7.3 %copy-start.25 = (f32[96,512]{1,0:T(8,128)S(1)}, f32[96,512]{1,0:T(8,128)}, u32[]{:S(2)}) copy-start(f32[96,512]{1,0:T(8,128)} %get-tuple-element.62) | copy-start | bytes 589828
  (25 other events, 64.1 us)

commit v3 on v2

--- a/solution.py
+++ b/solution.py
@@ -75,8 +75,8 @@
         acc[...] = acc[...] + line_got[away - 1]
 
 
-def line_gather(pos, count, buf, send, recv):
-    micro = buf.shape[0]
+def line_gather(pos, count, buf, send, recv, steps=None):
+    steps = range(buf.shape[0]) if steps is None else steps
     rows = buf.shape[1] // count
 
     def piece(block, step):
@@ -93,7 +93,7 @@
         )
 
     for hop in range(count):
-        for step in range(micro):
+        for step in steps:
             for way, target, block, can_send in (
                 (0, pos + 1, pos - hop, pos < count - 1),
                 (1, pos - 1, pos + hop, pos > 0),
@@ -114,7 +114,7 @@
 
         yield
     for hop in range(count - 1):
-        for step in range(micro):
+        for step in steps:
             for way, target, block, can_send in (
                 (0, pos + 1, pos - hop, pos < count - 1),
                 (1, pos - 1, pos + hop, pos > 0),
@@ -125,8 +125,8 @@
                     copy(block, step, target, way).wait_send()
 
 
-def line_scatter(pos, count, parts, got, staged, total, send, recv):
-    micro = parts.shape[0]
+def line_scatter(pos, count, parts, got, staged, total, send, recv, steps=None):
+    steps = range(parts.shape[0]) if steps is None else steps
     rows = parts.shape[1] // count
 
     def at(block):
@@ -149,7 +149,7 @@
         )
 
     for hop in range(count - 1, 0, -1):
-        for step in range(micro):
+        for step in steps:
             for way, target, block, there, has_input in ways(hop):
 
                 @pl.when(there & has_input)
@@ -167,7 +167,7 @@
                     copy(block, step, target, way).start()
 
         yield
-    for step in range(micro):
+    for step in steps:
         total[step] = parts[step, at(pos)].astype(jnp.float32)
         for way, target, block, there, has_input in ways(0):
 
@@ -177,7 +177,7 @@
                 total[step] = total[step] + got[way, step, at(pos)].astype(jnp.float32)
 
     for hop in range(count - 1, 0, -1):
-        for step in range(micro):
+        for step in steps:
             for way, target, block, there, has_input in ways(hop):
 
                 @pl.when(there)
@@ -404,17 +404,19 @@
             extra_all[step, own_rows(pos, extra_all, count)] = extra[step]
     greet(pos, count, me)
 
-    def main():
-        yield from line_scatter(pos, count, parts, got, staged, total_out, s_send, s_recv)
-        for step in range(parts.shape[0]):
-            total = total_out[step] + resid[step].astype(jnp.float32)
-            total_out[step] = total
-            normed_all[step, own_rows(pos, normed_all, count)] = norm_forward(
-                total, gain[...]
-            ).astype(jnp.bfloat16)
-        yield from line_gather(pos, count, normed_all, g_send, g_recv)
-
-    streams.append(main())
+    def main(step):
+        yield from line_scatter(
+            pos, count, parts, got, staged, total_out, s_send, s_recv, (step,)
+        )
+        total = total_out[step] + resid[step].astype(jnp.float32)
+        total_out[step] = total
+        normed_all[step, own_rows(pos, normed_all, count)] = norm_forward(
+            total, gain[...]
+        ).astype(jnp.bfloat16)
+        yield from line_gather(pos, count, normed_all, g_send, g_recv, (step,))
+
+    for step in range(parts.shape[0]):
+        streams.append(main(step))
     if beside == "cube":
         streams.append(cube_gather(me, extra_all, refs[6], refs[7]))
     if beside == "line":
@@ -436,16 +438,18 @@
     me = lax.axis_index("dp") if cubes else None
     greet(pos, count, me)
 
-    def main():
-        yield from line_scatter(pos, count, parts, got, staged, grad_out, s_send, s_recv)
-        gain_out[...] = jnp.zeros_like(gain_out)
-        for step in range(parts.shape[0]):
-            moved, gain_part = norm_backward(grad_out[step], values[step], gain[...])
-            total = grad_in[step].astype(jnp.float32) + moved
-            grad_out[step] = total
-            gain_out[...] = gain_out[...] + gain_part
-            gathered[step, own_rows(pos, gathered, count)] = total.astype(jnp.bfloat16)
-        yield from line_gather(pos, count, gathered, g_send, g_recv)
+    gain_out[...] = jnp.zeros_like(gain_out)
+
+    def main(step):
+        yield from line_scatter(
+            pos, count, parts, got, staged, grad_out, s_send, s_recv, (step,)
+        )
+        moved, gain_part = norm_backward(grad_out[step], values[step], gain[...])
+        total = grad_in[step].astype(jnp.float32) + moved
+        grad_out[step] = total
+        gain_out[...] = gain_out[...] + gain_part
+        gathered[step, own_rows(pos, gathered, count)] = total.astype(jnp.bfloat16)
+        yield from line_gather(pos, count, gathered, g_send, g_recv, (step,))
 
     def side():
         yield from line_scatter(
@@ -457,7 +461,7 @@
             else:
                 side_out[step] = side_total[step]
 
-    run_together(main(), side(), *cube_streams(me, weight_parts, weight_out, refs))
+    run_together(*[main(step) for step in range(parts.shape[0])], side(), *cube_streams(me, weight_parts, weight_out, refs))
 
 
 def cube_streams(me, weight_parts, weight_out, refs):
@@ -501,17 +505,19 @@
     me = lax.axis_index("dp") if cubes else None
     greet(pos, count, me)
 
-    def main():
-        yield from line_scatter(pos, count, parts, got, staged, grad_out, s_send, s_recv)
-        small_out[...] = small[...]
-        for step in range(parts.shape[0]):
-            moved, gain_part = norm_backward(
-                grad_out[step], values[step].astype(jnp.float32), gain[...]
-            )
-            grad_out[step] = grad_in[step] + moved
-            small_out[0:1] = small_out[0:1] + gain_part
-
-    run_together(main(), *cube_streams(me, weight_parts, weight_out, refs))
+    small_out[...] = small[...]
+
+    def main(step):
+        yield from line_scatter(
+            pos, count, parts, got, staged, grad_out, s_send, s_recv, (step,)
+        )
+        moved, gain_part = norm_backward(
+            grad_out[step], values[step].astype(jnp.float32), gain[...]
+        )
+        grad_out[step] = grad_in[step] + moved
+        small_out[0:1] = small_out[0:1] + gain_part
+
+    run_together(*[main(step) for step in range(parts.shape[0])], *cube_streams(me, weight_parts, weight_out, refs))
     if cubes:
         small_sum(pos, count, me, small_out, *refs[10 * cubes :])
 

time: 302 us -> 298 us (0.987)
  Pallas kernels: 216 us -> 211 us
    pallas_call x6, Pallas kernels: 212 us -> 207 us  [call(): pl.pallas_call(kernel, out_shape=[jax.ShapeDtypeStruct(shape, kind) for s...]
where the time goes in v3:
time: 298 us; the launch traced here: 297 us
  Pallas kernels  211 us (71%)
  matrix products  51.8 us (17%)
  local copies, waits for them, and re-layouts  24.9 us (8%)
  other arithmetic  7.39 us (2%)
    pallas_call x6, Pallas kernels, call(): pl.pallas_call(kernel, out_shape=[jax.ShapeDtypeStruct(shape, kind) for s...  207 us
    dot_general x7, matrix products, rows_dot_t(): lax.dot_general(rows, matrix, (((2,), (1,)), ((), ())), preferred_element...  11.7 us
    dot_general x7, matrix products, rows_dot(): lax.dot_general(rows, matrix, (((2,), (0,)), ((), ())), preferred_element...  10.6 us
    dot_general x7, matrix products, dot_left_t(): lax.dot_general(left, right, (((0,), (0,)), ((), ())), preferred_element_...  9.49 us
    unnamed x111, local copies, waits for them, and re-layouts  8.34 us

profile of v3, /device:TPU:0, one launch (start us, length us, event | category | flops | bytes accessed | tf_op | source)
XLA Modules:
  0.0 296.5 jit_solution(11448966675929259694)
XLA Ops:
  3.3 1.8 concatenate.24.refs_0_
  5.1 28.8 %entry_gather.1 = (bf16[8,96,1664]{2,1,0:T(8,128)(2,1)}, bf16[2,256,768]{2,1,0:T(8,128)(2,1)}, bf16[2,128,768]{2,1,0:T(8,128)(2,1)}) custom-call(bf16[96,1664]{1,0:T(8,128)(2,1)} %concatenate.24.refs_0_, bf16[2,64,768]{2,1,0:T(8,128)(2,1)} %refs_1_.5, bf16[2,32,768]{2,1,0:T(8,128)(2,1)} %refs_2_.1), custom_call_target="tpu_custom_call" | custom-call | tf_op jit(solution)/shard_map/entry_gather/pallas_call | solution.py:349
  37.1 2.0 convolution_convert_fusion.6
  41.5 1.8 bias_spread.1
  43.5 3.1 %fusion.48 = (f32[2,3,256]{2,1,0:T(4,128)S(1)}, f32[2,3,256,256]{3,2,1,0:T(8,128)}) fusion(bf16[2,256,3,64]{1,3,2,0:T(8,128)(2,1)S(1)} %bitcast.194, bf16[2,256,3,64]{1,3,2,0:T(8,128)(2,1)S(1)} %bitcast.190, f32[3,256,256]{2,1,0:T(8,128)} %bias_spread.1, pred[2,256,256]{2,1,0:T(8,128)(4,1)S(1)} %compare_and_fusion), kind=kOutput, calls=%fused_computation.118 | convolution fusion | flops 51904768 | bytes 2889728 | tf_op jit(solution)/shard_map/sub | solution.py:561
  46.6 2.3 convolution_convert_fusion.16
  50.2 1.8 pad_maximum_fusion.5.refs_3_
  51.9 32.7 %self_sum_norm.1 = (f32[2,64,768]{2,1,0:T(8,128)}, bf16[2,256,768]{2,1,0:T(8,128)(2,1)}, bf16[8,96,1536]{2,1,0:T(8,128)(2,1)}) custom-call(bf16[2,256,768]{2,1,0:T(8,128)(2,1)} %convolution_convert_fusion.5.refs_0_, bf16[2,64,768]{2,1,0:T(8,128)(2,1)} %refs_1_.5, f32[1,768]{1,0:T(1,128)} %get-tuple-element.142.refs_2_.refs_3_, ...), custom_call_target="tpu_custom_call" | custom-call | tf_op jit(solution)/shard_map/self_sum_norm/pallas_call | solution.py:349
  84.6 1.7 convolution_convert_fusion.12
  88.4 2.9 fusion.49
  94.3 36.3 %cross_sum_norm.1 = (f32[2,64,768]{2,1,0:T(8,128)}, bf16[2,256,768]{2,1,0:T(8,128)(2,1)}, bf16[2,256,768]{2,1,0:T(8,128)(2,1)}) custom-call(bf16[2,256,768]{2,1,0:T(8,128)(2,1)} %convolution_convert_fusion.4.refs_0_, f32[2,64,768]{2,1,0:T(8,128)} %get-tuple-element.45.refs_1_.refs_2_, f32[1,768]{1,0:T(1,128)} %get-tuple-element.141.refs_2_.refs_3_, ...), custom_call_target="tpu_custom_call" | custom-call | tf_op jit(solution)/shard_map/cross_sum_norm/pallas_call | solution.py:349
  130.7 2.2 fusion.13
  135.7 1.9 convolution_convert_fusion.3.refs_0_
  137.6 37.9 %feed_back.1 = (f32[2,64,768]{2,1,0:T(8,128)}, bf16[2,256,768]{2,1,0:T(8,128)(2,1)}, bf16[2,64,768]{2,1,0:T(8,128)(2,1)}, f32[1,768]{1,0:T(1,128)}) custom-call(bf16[2,256,768]{2,1,0:T(8,128)(2,1)} %convolution_convert_fusion.3.refs_0_, bf16[2,256,768]{2,1,0:T(8,128)(2,1)} %convolution_convert_fusion.2.refs_1_, ...), custom_call_target="tpu_custom_call" | custom-call | tf_op jit(solution)/shard_map/feed_back/pallas_call | solution.py:349
  181.9 2.2 convolution_convert_fusion.18
  187.5 2.8 bitcast_convert_fusion.2
  190.3 2.1 bitcast_convert_fusion
  195.1 38.5 %cross_back.1 = (f32[2,64,768]{2,1,0:T(8,128)}, bf16[2,256,768]{2,1,0:T(8,128)(2,1)}, f32[2,32,768]{2,1,0:T(8,128)}, f32[1,768]{1,0:T(1,128)}, f32[96,1024]{1,0:T(8,128)}, /*index=5*/f32[96,512]{1,0:T(8,128)}) custom-call(bf16[2,256,768]{2,1,0:T(8,128)(2,1)} %convolution_convert_fusion.1.refs_0_, bf16[2,128,768]{2,1,0:T(8,128)(2,1)} %convolution_convert_fusion.7.refs_1_, ...), custom_call_target="tpu_custom_call" | custom-call | tf_op jit(solution)/shard_map/cross_back/pallas_call | solution.py:349
  238.7 2.2 multiply_reduce_fusion
  242.1 2.2 convolution_convert_fusion.13
  246.4 2.2 diagonal_sums.1
  250.6 2.9 convolution_convert_fusion.refs_0_
  253.6 32.7 %exit_sums.1 = (f32[2,64,768]{2,1,0:T(8,128)}, f32[8,768]{1,0:T(8,128)}, f32[96,576]{1,0:T(8,128)}, f32[96,960]{1,0:T(8,128)}) custom-call(bf16[2,256,768]{2,1,0:T(8,128)(2,1)} %convolution_convert_fusion.refs_0_, bf16[2,64,768]{2,1,0:T(8,128)(2,1)} %refs_1_.5, f32[1,768]{1,0:T(1,128)} %get-tuple-element.139.refs_2_, ...), custom_call_target="tpu_custom_call" | custom-call | tf_op jit(solution)/shard_map/exit_sums/pallas_call | solution.py:349
  286.3 2.2 slice_bitcast_fusion.21
  (169 shorter events, 47.8 us)
Async XLA Ops:
  0.7 40.0 %copy-start = (bf16[32,3]{0,1:T(4,128)(2,1)S(1)}, bf16[32,3]{0,1:T(4,128)(2,1)}, u32[]{:S(2)}) copy-start(bf16[32,3]{0,1:T(4,128)(2,1)} %param.41) | copy-start | bytes 580
  39.2 7.4 %copy-start.22 = (bf16[2,256,192]{1,2,0:T(8,128)(2,1)}, bf16[2,256,192]{1,2,0:T(8,128)(2,1)S(1)}, u32[]{:S(2)}) copy-start(bf16[2,256,192]{1,2,0:T(8,128)(2,1)S(1)} %get-tuple-element.123) | copy-start | bytes 589828
  40.7 5.9 %copy-start.39 = (s32[256]{0:T(256)}, s32[256]{0:T(256)S(1)}, u32[]{:S(2)}) copy-start(s32[256]{0:T(256)S(1)} %pad_add_fusion) | copy-start | bytes 3076
  43.5 5.4 %copy-start.28 = (pred[2,256,256]{2,1,0:T(8,128)(4,1)}, pred[2,256,256]{2,1,0:T(8,128)(4,1)S(1)}, u32[]{:S(2)}) copy-start(pred[2,256,256]{2,1,0:T(8,128)(4,1)S(1)} %compare_and_fusion) | copy-start | bytes 393220
  48.8 35.8 %copy-start.10 = (bf16[2,3,64,256]{3,2,1,0:T(8,128)(2,1)}, bf16[2,3,64,256]{3,2,1,0:T(8,128)(2,1)S(1)}, u32[]{:S(2)}) copy-start(bf16[2,3,64,256]{3,2,1,0:T(8,128)(2,1)S(1)} %convolution_convert_fusion.16) | copy-start | bytes 589828
  50.2 36.2 %copy-start.18 = (bf16[2,128,768]{2,1,0:T(8,128)(2,1)S(1)}, bf16[2,128,768]{2,1,0:T(8,128)(2,1)}, u32[]{:S(2)}) copy-start(bf16[2,128,768]{2,1,0:T(8,128)(2,1)} %get-tuple-element.41) | copy-start | bytes 1179652
  86.3 44.3 %copy-start.14 = (bf16[2,256,192]{1,2,0:T(8,128)(2,1)}, bf16[2,256,192]{1,2,0:T(8,128)(2,1)S(1)}, u32[]{:S(2)}) copy-start(bf16[2,256,192]{1,2,0:T(8,128)(2,1)S(1)} %convolution_convert_fusion.12) | copy-start | bytes 589828
  92.8 40.0 %copy-start.12 = (bf16[2,3,64,256]{3,2,1,0:T(8,128)(2,1)}, bf16[2,3,64,256]{3,2,1,0:T(8,128)(2,1)S(1)}, u32[]{:S(2)}) copy-start(bf16[2,3,64,256]{3,2,1,0:T(8,128)(2,1)S(1)} %convolution_convert_fusion.11) | copy-start | bytes 589828
  92.8 37.8 %copy-start.41 = (bf16[8,96,1536]{2,1,0:T(8,128)(2,1)S(1)}, bf16[8,96,1536]{2,1,0:T(8,128)(2,1)}, u32[]{:S(2)}) copy-start(bf16[8,96,1536]{2,1,0:T(8,128)(2,1)} %get-tuple-element.47) | copy-start | bytes 7077892
  137.6 39.7 %copy-start.9 = (f32[2,3,256,128]{2,3,1,0:T(8,128)S(1)}, f32[2,3,256,128]{2,3,1,0:T(8,128)}, u32[]{:S(2)}) copy-start(f32[2,3,256,128]{2,3,1,0:T(8,128)} %get-tuple-element.146) | copy-start | bytes 2359300
  137.6 39.7 %copy-start.30 = (f32[2,3,256]{2,1,0:T(4,128)S(1)}, f32[2,3,256]{2,1,0:T(4,128)}, u32[]{:S(2)}) copy-start(f32[2,3,256]{2,1,0:T(4,128)} %get-tuple-element.145) | copy-start | bytes 18436
  185.8 4.5 %copy-start.42 = (bf16[2,256,768]{2,1,0:T(8,128)(2,1)S(1)}, bf16[2,256,768]{2,1,0:T(8,128)(2,1)}, u32[]{:S(2)}) copy-start(bf16[2,256,768]{2,1,0:T(8,128)(2,1)} %get-tuple-element.48) | copy-start | bytes 2359300
  185.8 4.5 %copy-start.46 = (bf16[2,256,512]{2,1,0:T(8,128)(2,1)S(1)}, bf16[2,256,512]{2,1,0:T(8,128)(2,1)}, u32[]{:S(2)}) copy-start(bf16[2,256,512]{2,1,0:T(8,128)(2,1)} %copy-done.45) | copy-start | bytes 1572868
  185.8 4.5 %copy-start.48 = (bf16[2,256,512]{2,1,0:T(8,128)(2,1)S(1)}, bf16[2,256,512]{2,1,0:T(8,128)(2,1)}, u32[]{:S(2)}) copy-start(bf16[2,256,512]{2,1,0:T(8,128)(2,1)} %copy-done.47) | copy-start | bytes 1572868
  195.1 38.5 %copy-start.11 = (bf16[2,3,64,256]{3,2,1,0:T(8,128)(2,1)S(1)}, bf16[2,3,64,256]{3,2,1,0:T(8,128)(2,1)}, u32[]{:S(2)}) copy-start(bf16[2,3,64,256]{3,2,1,0:T(8,128)(2,1)} %copy-done.10) | copy-start | bytes 589828
  195.1 40.0 %copy-start.2 = (bf16[2,256,768]{2,1,0:T(8,128)(2,1)S(1)}, bf16[2,256,768]{2,1,0:T(8,128)(2,1)}, u32[]{:S(2)}) copy-start(bf16[2,256,768]{2,1,0:T(8,128)(2,1)} %get-tuple-element.51) | copy-start | bytes 2359300
  195.1 40.0 %copy-start.13 = (bf16[2,3,64,256]{3,2,1,0:T(8,128)(2,1)S(1)}, bf16[2,3,64,256]{3,2,1,0:T(8,128)(2,1)}, u32[]{:S(2)}) copy-start(bf16[2,3,64,256]{3,2,1,0:T(8,128)(2,1)} %copy-done.12) | copy-start | bytes 589828
  245.1 4.9 %copy-start.33 = (f32[1,768]{1,0:T(1,128)S(1)}, f32[1,768]{1,0:T(1,128)}, u32[]{:S(2)}) copy-start(f32[1,768]{1,0:T(1,128)} %get-tuple-element.56) | copy-start | bytes 9220
  245.1 4.9 %copy-start.34 = (f32[1,768]{1,0:T(1,128)S(1)}, f32[1,768]{1,0:T(1,128)}, u32[]{:S(2)}) copy-start(f32[1,768]{1,0:T(1,128)} %get-tuple-element.55) | copy-start | bytes 9220
  286.3 6.7 %copy-start.19 = (f32[96,1024]{1,0:T(8,128)S(1)}, f32[96,1024]{1,0:T(8,128)}, u32[]{:S(2)}) copy-start(f32[96,1024]{1,0:T(8,128)} %get-tuple-element.61) | copy-start | bytes 1179652
  286.3 7.4 %copy-start.24 = (bf16[2,64,768]{2,1,0:T(8,128)(2,1)S(1)}, bf16[2,64,768]{2,1,0:T(8,128)(2,1)}, u32[]{:S(2)}) copy-start(bf16[2,64,768]{2,1,0:T(8,128)(2,1)} %get-tuple-element.172) | copy-start | bytes 589828
  286.3 8.1 %copy-start.20 = (f32[2,64,768]{2,1,0:T(8,128)S(1)}, f32[2,64,768]{2,1,0:T(8,128)}, u32[]{:S(2)}) copy-start(f32[2,64,768]{2,1,0:T(8,128)} %get-tuple-element.173) | copy-start | bytes 1179652
  288.5 6.6 %copy-start.26 = (f32[2,32,768]{2,1,0:T(8,128)S(1)}, f32[2,32,768]{2,1,0:T(8,128)}, u32[]{:S(2)}) copy-start(f32[2,32,768]{2,1,0:T(8,128)} %get-tuple-element.174) | copy-start | bytes 589828
  288.6 7.3 %copy-start.25 = (f32[96,512]{1,0:T(8,128)S(1)}, f32[96,512]{1,0:T(8,128)}, u32[]{:S(2)}) copy-start(f32[96,512]{1,0:T(8,128)} %get-tuple-element.62) | copy-start | bytes 589828
  (25 other events, 64.1 us)
